TPU v7x, 512 devices: a whole 4x8x8 slice. The times are simulated.
512 devices in a mesh: sp: 32 (over x, z_lo, core), ch: 16 (over y, z_hi).
Axes of the slice: x: 4, y: 8, z: 8 (z_hi: 2, z_lo: 4; z = z_hi * 4 + z_lo), core: 2. Of those that a mesh axis runs over, the one named last changes fastest.
Arguments:
- volume: bfloat16 [256, 64, 8, 128], P('ch', 'sp'), may hold values from -6 to 6
- filters: bfloat16 [256, 3, 3, 3, 256], P('ch'), may hold values from -0.078125 to 0.078125
- cotangent: bfloat16 [256, 64, 8, 128], P('ch', 'sp'), may hold values from -6 to 6
Outputs:
- response: bfloat16 [256, 64, 8, 128], P('ch', 'sp')
- input_grad: bfloat16 [256, 64, 8, 128], P('ch', 'sp')
- filter_grad: bfloat16 [256, 3, 3, 3, 256], P('ch')
All inputs are finite; a program needn't handle non-finite values.
Results may differ from a plain program's by a relative error of at most 0.0024.
Values may be sent and summed in bfloat16 or wider, within the bound.
No kernel may reach another device: no remote copies, remote signals or barrier semaphores. Data moves between devices by JAX's collectives and lax.ppermute only.
A program may use at most 64 MiB of HBM per device.

v0:
```python
import math

import jax
import jax.numpy as jnp
from jax import lax
from jax.sharding import PartitionSpec as P


def extended(value, sides, width):
    for axis, dim in sides:
        size, length = (lax.axis_size(axis), value.shape[dim])
        up = [(i, (i + 1) % size) for i in range(size - 1)]
        down = [(j, i) for i, j in up]
        last = lax.slice_in_dim(value, length - width, length, axis=dim)
        first = lax.slice_in_dim(value, 0, width, axis=dim)
        before = lax.ppermute(last, axis, up)
        after = lax.ppermute(first, axis, down)
        value = jnp.concatenate([before, value, after], axis=dim)
    return value


def place_taps(total, product, flipped):
    height = total.shape[2]
    width = total.shape[3]
    padded = jnp.pad(product, ((0, 0), (0, 0), (0, 0), (0, 0), (1, 1), (1, 1)))
    for row_tap in range(3):
        for col_tap in range(3):
            row_from = 2 - row_tap if flipped else row_tap
            col_from = 2 - col_tap if flipped else col_tap
            total = (
                total
                + padded[
                    row_tap,
                    col_tap,
                    :,
                    :,
                    row_from : row_from + height,
                    col_from : col_from + width,
                ]
            )
    return total


def forward_terms(filters, total, piece):
    count = piece.shape[0]
    outputs = filters.shape[0]
    depth, height, width = (total.shape[1], total.shape[2], total.shape[3])
    for depth_tap in range(3):
        rows = piece[:, depth_tap : depth_tap + depth].reshape(count, -1)
        taps = jnp.transpose(filters[:, depth_tap], (1, 2, 3, 0)).reshape(9, count, outputs)
        product = lax.dot_general(
            taps, rows, (((1,), (0,)), ((), ())), preferred_element_type=jnp.float32
        )
        total = place_taps(total, product.reshape(3, 3, outputs, depth, height, width), False)
    return total


def data_terms(swapped, total, piece):
    count = piece.shape[0]
    channels = swapped.shape[4]
    depth, height, width = (total.shape[1], total.shape[2], total.shape[3])
    for depth_tap in range(3):
        rows = piece[:, 2 - depth_tap : 2 - depth_tap + depth].reshape(count, -1)
        taps = jnp.transpose(swapped[:, depth_tap], (1, 2, 3, 0)).reshape(9, channels, count)
        product = lax.dot_general(
            taps, rows, (((2,), (0,)), ((), ())), preferred_element_type=jnp.float32
        )
        total = place_taps(total, product.reshape(3, 3, channels, depth, height, width), True)
    return total


def filter_terms(shifted, depth, piece):
    count = piece.shape[0]
    outputs = shifted.shape[1]
    blocks = []
    for depth_tap in range(3):
        rows = piece[:, depth_tap : depth_tap + depth].reshape(count, -1)
        block = lax.dot_general(
            rows, shifted, (((1,), (2,)), ((), ())), preferred_element_type=jnp.float32
        )
        blocks.append(jnp.transpose(block, (2, 1, 0)).reshape(outputs, 3, 3, count))
    return jnp.stack(blocks, axis=1)


def local(volume, filters, cotangent):
    depth, height, width = (volume.shape[1], volume.shape[2], volume.shape[3])
    outputs = filters.shape[0]
    local_chan = volume.shape[0]
    planes_all = depth * lax.axis_size("sp")
    rimmed = extended(volume, (("sp", 1),), 1)
    grad_padded = jnp.pad(cotangent, ((0, 0), (0, 0), (1, 1), (1, 1)))
    shifted = jnp.stack(
        [
            grad_padded[
                :, :, 2 - row_tap : 2 - row_tap + height, 2 - col_tap : 2 - col_tap + width
            ].reshape(outputs, -1)
            for row_tap in range(3)
            for col_tap in range(3)
        ]
    )
    start_resp = jnp.zeros((outputs, depth, height, width), jnp.float32)
    response_sum = forward_terms(
        filters, start_resp, lax.all_gather(rimmed, "ch", axis=0, tiled=True)
    )
    kernel_part = filter_terms(shifted, depth, lax.all_gather(rimmed, "ch", axis=0, tiled=True))
    swapped = lax.all_to_all(filters, "ch", split_axis=4, concat_axis=0, tiled=True)
    start_data = jnp.zeros((local_chan, depth, height, width), jnp.float32)
    grad_rimmed = extended(cotangent, (("sp", 1),), 1)
    data_sum = data_terms(
        swapped, start_data, lax.all_gather(grad_rimmed, "ch", axis=0, tiled=True)
    )
    kernel_total = lax.psum(kernel_part, "sp")
    factor = 1.0 / math.sqrt(planes_all * height * width)
    return (
        response_sum.astype(jnp.bfloat16),
        data_sum.astype(jnp.bfloat16),
        (kernel_total * factor).astype(jnp.bfloat16),
    )


def solution(mesh):
    in_specs = (
        P("ch", "sp", None, None),
        P("ch", None, None, None, None),
        P("ch", "sp", None, None),
    )
    out_specs = (
        P("ch", "sp", None, None),
        P("ch", "sp", None, None),
        P("ch", None, None, None, None),
    )
    return jax.shard_map(local, mesh=mesh, in_specs=in_specs, out_specs=out_specs, check_vma=False)
```

profile of v0, /device:TPU:1, one launch (start us, length us, event | category | flops | bytes accessed | tf_op | source)
XLA Modules:
  0.0 524.1 jit_solution(11226652834129641765)
XLA Ops:
  7.2 0.8 fusion.82
  8.1 5.4 %collective-permute-start.2 = (bf16[16,1,8,128]{3,2,1,0:T(8,128)(2,1)S(1)}, bf16[16,1,8,128]{3,2,1,0:T(8,128)(2,1)S(1)}, u32[]{:S(2)}, u32[]{:S(2)}) collective-permute-start(bf16[16,1,8,128]{3,2,1,0:T(8,128)(2,1)S(1)} %get-tuple-element.23), channel_id=1, source_target_pairs={{0,16},{16,32},{32,48},{48,64},{64,80},{80,96},{96,112},{112,128},... | collective-permute-start | bytes 98312 | tf_op jit(solution)/shard_map/ppermute | solution.py:16
  13.4 4.7 collective-permute-start.3
  18.1 0.8 collective-permute-done.3
  19.0 1.5 pad_maximum_fusion.2
  20.6 0.8 fusion.83
  21.4 1.9 collective-permute-start
  23.3 2.4 collective-permute-start.1
  25.7 3.3 collective-permute-done.1
  28.9 1.5 pad_maximum_fusion.1
  30.5 1.8 copy.7
  32.4 2.9 reshape.131
  35.2 13.7 %all-to-all-start = ((bf16[16,2,3456]{2,1,0:T(2,128)(2,1)}), bf16[16,2,3456]{2,1,0:T(2,128)(2,1)S(1)}, u32[]{:S(2)}, u32[]{:S(2)}) async-start(bf16[16,2,3456]{2,1,0:T(2,128)(2,1)} %reshape.131), calls=%async_computation | async-start | bytes 442368 | tf_op jit(solution)/shard_map/all_to_all | solution.py:106
  49.7 0.8 copy-done.10
  50.5 14.2 %all-to-all-done = bf16[16,2,3456]{2,1,0:T(2,128)(2,1)S(1)} async-done(((bf16[16,2,3456]{2,1,0:T(2,128)(2,1)}), bf16[16,2,3456]{2,1,0:T(2,128)(2,1)S(1)}, u32[]{:S(2)}, u32[]{:S(2)}) %all-to-all-start) | async-done | bytes 221216 | tf_op jit(solution)/shard_map/all_to_all | solution.py:106
  64.7 2.2 reshape.132
  67.0 2.7 copy.8
  69.6 2.8 all_to_all.16
  72.4 0.7 fusion.80
  73.1 55.9 %all-gather.5.cloned.1.call-done = bf16[256,4,8,128]{3,2,1,0:T(8,128)(2,1)} async-done(((bf16[16,4,8,128]{3,2,1,0:T(8,128)(2,1)}), bf16[256,4,8,128]{3,2,1,0:T(8,128)(2,1)}) %all-gather.5.cloned.1.call-update) | async-done | bytes 2097168 | tf_op jit(solution)/shard_map/all_gather | solution.py:110
  129.0 2.4 fusion.78
  131.4 1.3 reshape.119
  132.6 1.3 reshape.121
  133.9 1.2 reshape.120
  135.2 96.8 %all-gather.3.cloned.1.call-done = bf16[256,4,8,128]{3,2,1,0:T(8,128)(2,1)} async-done(((bf16[16,4,8,128]{3,2,1,0:T(8,128)(2,1)}), bf16[256,4,8,128]{3,2,1,0:T(8,128)(2,1)}) %all-gather.3.cloned.1.call-update) | async-done | bytes 2097168 | tf_op jit(solution)/shard_map/all_gather | solution.py:103
  232.0 2.4 fusion.79
  234.4 1.3 reshape.122
  235.7 1.3 reshape.124
  237.0 2.0 fusion.87
  239.0 1.2 fusion.89
  240.1 1.3 reshape.123
  241.4 1.9 fusion.88
  243.3 0.8 pad_maximum_fusion
  244.2 0.3 convolution_bitcast_fusion.1
  244.5 0.2 copy.12
  244.7 0.3 convolution_bitcast_fusion
  245.3 0.3 convolution_bitcast_fusion.2
  245.6 0.2 copy.10
  245.9 1.0 copy-done.2
  246.9 0.3 fusion.86
  247.2 0.2 copy.17
  247.4 1.0 copy-done.1
  248.4 0.3 fusion.84
  249.0 1.0 copy-done
  250.0 0.3 fusion.85
  250.5 1.9 fusion.76
  252.5 263.4 %all-reduce.9.cloned.1.call-done = f32[16,3,3,3,256]{4,0,3,2,1:T(8,128)} async-done(((f32[16,3,3,3,256]{4,0,3,2,1:T(8,128)}), f32[16,3,3,3,256]{4,0,3,2,1:T(8,128)}) %all-reduce.9.cloned.1.call-update) | async-done | bytes 442384 | tf_op jit(solution)/shard_map/psum | solution.py:112
  515.8 1.7 multiply_convert_fusion
  (51 shorter events, 1.4 us)
Async XLA Ops:
  7.2 23.3 %copy-start.5 = (bf16[16,3,3,3,256]{4,0,3,2,1:T(8,128)(2,1)S(1)}, bf16[16,3,3,3,256]{4,0,3,2,1:T(8,128)(2,1)}, u32[]{:S(2)}) copy-start(bf16[16,3,3,3,256]{4,0,3,2,1:T(8,128)(2,1)} %param.4) | copy-start | bytes 663556
  7.2 121.8 %all-gather.5.cloned.1.call-start = ((), (), s32[]{:S(2)}) async-start(), calls=%async_computation.2 | async-start | bytes 2228224 | tf_op jit(solution)/shard_map/all_gather | solution.py:110
  8.1 10.1 %collective-permute-start.2 = (bf16[16,1,8,128]{3,2,1,0:T(8,128)(2,1)S(1)}, bf16[16,1,8,128]{3,2,1,0:T(8,128)(2,1)S(1)}, u32[]{:S(2)}, u32[]{:S(2)}) collective-permute-start(bf16[16,1,8,128]{3,2,1,0:T(8,128)(2,1)S(1)} %get-tuple-element.23), channel_id=1, source_target_pairs={{0,16},{16,32},{32,48},{48,64},{64,80},{80,96},{96,112},{112,128},... | collective-permute-start | bytes 98312 | tf_op jit(solution)/shard_map/ppermute | solution.py:16
  13.4 5.5 %collective-permute-start.3 = (bf16[16,1,8,128]{3,2,1,0:T(8,128)(2,1)S(1)}, bf16[16,1,8,128]{3,2,1,0:T(8,128)(2,1)S(1)}, u32[]{:S(2)}, u32[]{:S(2)}) collective-permute-start(bf16[16,1,8,128]{3,2,1,0:T(8,128)(2,1)S(1)} %get-tuple-element.24), channel_id=1, source_target_pairs={{16,0},{32,16},{48,32},{64,48},{80,64},{96,80},{112,96},{128,112},... | collective-permute-start | bytes 98312 | tf_op jit(solution)/shard_map/ppermute | solution.py:17
  20.5 211.5 %all-gather.3.cloned.1.call-start = ((), (), s32[]{:S(2)}) async-start(), calls=%async_computation.1 | async-start | bytes 2228224 | tf_op jit(solution)/shard_map/all_gather | solution.py:103
  21.4 4.3 collective-permute-start
  23.3 5.7 %collective-permute-start.1 = (bf16[16,1,8,128]{3,2,1,0:T(8,128)(2,1)S(1)}, bf16[16,1,8,128]{3,2,1,0:T(8,128)(2,1)S(1)}, u32[]{:S(2)}, u32[]{:S(2)}) collective-permute-start(bf16[16,1,8,128]{3,2,1,0:T(8,128)(2,1)S(1)} %get-tuple-element.26), channel_id=1, source_target_pairs={{16,0},{32,16},{48,32},{64,48},{80,64},{96,80},{112,96},{128,112},... | collective-permute-start | bytes 98312 | tf_op jit(solution)/shard_map/ppermute | solution.py:17
  32.3 16.7 %copy-start.4 = (bf16[16,2,8,128]{3,2,1,0:T(8,128)(2,1)S(1)}, bf16[16,2,8,128]{3,2,1,0:T(8,128)(2,1)}, u32[]{:S(2)}) copy-start(bf16[16,2,8,128]{3,2,1,0:T(8,128)(2,1)} %param.5) | copy-start | bytes 196612
  35.2 29.5 %all-to-all-start = ((bf16[16,2,3456]{2,1,0:T(2,128)(2,1)}), bf16[16,2,3456]{2,1,0:T(2,128)(2,1)S(1)}, u32[]{:S(2)}, u32[]{:S(2)}) async-start(bf16[16,2,3456]{2,1,0:T(2,128)(2,1)} %reshape.131), calls=%async_computation | async-start | bytes 442368 | tf_op jit(solution)/shard_map/all_to_all | solution.py:106
  49.0 466.9 %all-reduce.9.cloned.1.call-start = ((), (), s32[]{:S(2)}) async-start(), calls=%async_computation.3 | async-start | bytes 884736 | tf_op jit(solution)/shard_map/psum | solution.py:112
  49.7 0.8 copy-start.10
  236.9 2.0 copy-start.3
  237.0 2.0 copy-start.11
  241.4 1.9 copy-start.6
  245.6 1.2 copy-start.2
  245.6 1.2 copy-start.9
  247.2 1.2 copy-start.1
  247.2 1.2 copy-start.8
  248.7 1.2 copy-start
  248.8 1.2 copy-start.7
Sparse Core Ops, SparseCore 0:
  20.6 108.2 all-gather.4
  132.2 99.7 all-gather.2
  244.3 271.4 all-reduce.8
where the time goes:
time: 525 us; the launch traced here: 524 us
  waiting for transfers between devices  434 us (83%)
  local copies, waits for them, and re-layouts  32.7 us (6%)
  starting transfers between devices  28.2 us (5%)
  between operations  14.2 us (3%)
  other arithmetic  7.52 us (1%)
  matrix products  7.03 us (1%)
    psum x1, waiting for transfers between devices, local(): kernel_total = lax.psum(kernel_part, 'sp')  263 us
    all_gather x1, waiting for transfers between devices, local(): lax.all_gather(rimmed, 'ch', axis=0, tiled=True)  96.8 us
    all_gather x1, waiting for transfers between devices, local(): lax.all_gather(grad_rimmed, 'ch', axis=0, tiled=True)  55.9 us
    all_to_all x1, waiting for transfers between devices, local(): lax.all_to_all(filters, 'ch', split_axis=4, concat_axis=0, tiled=True)  14.2 us
    all_to_all x1, starting transfers between devices, local(): lax.all_to_all(filters, 'ch', split_axis=4, concat_axis=0, tiled=True)  13.7 us
    unnamed x41, local copies, waits for them, and re-layouts  12 us
  transfers between devices with their start and end apart: 8, of which 6 were waited for; matrix products, arithmetic and copies ran while one was open for 5% of the time, Pallas kernels for 0%

commit v1 on v0

v1 whole, which is shorter than its diff:
```python
import math

import jax
import jax.numpy as jnp
from jax import lax
from jax.experimental import pallas as pl
from jax.experimental.pallas import tpu as pltpu
from jax.sharding import Mesh
from jax.sharding import PartitionSpec as P

BF = jnp.bfloat16
F32 = jnp.float32
VMEM = pl.BlockSpec(memory_space=pltpu.VMEM)
SMEM = pl.BlockSpec(memory_space=pltpu.SMEM)
PARAMS = pltpu.CompilerParams(vmem_limit_bytes=48 * 1024 * 1024)


def call(kernel, out_shape, in_specs, scratch=()):
    return pl.pallas_call(
        kernel,
        out_shape=out_shape,
        in_specs=in_specs,
        out_specs=jax.tree.map(lambda _: VMEM, out_shape),
        scratch_shapes=list(scratch),
        compiler_params=PARAMS,
    )


def lane_half(shape):
    return lax.broadcasted_iota(jnp.int32, shape, len(shape) - 1) < 64


def pack_kernel(fil, out):
    low = lane_half((16, 128))
    for r in range(14):
        for half in range(2):
            lanes = pl.ds(128 * half, 128)
            first = fil[2 * r, :, lanes].astype(F32)
            if r < 13:
                second = fil[2 * r + 1, :, lanes].astype(F32)
            else:
                second = jnp.zeros_like(first)
            even = jnp.where(low, first, pltpu.roll(second, 64, 1))
            odd = jnp.where(low, pltpu.roll(first, 64, 1), second)
            out[2 * half, r] = even.astype(BF)
            out[2 * half + 1, r] = odd.astype(BF)


def put(dst, slot, row, block):
    wide = block.astype(F32)
    lane = lax.broadcasted_iota(jnp.int32, (64, 128), 1)
    dst[slot, row, 0] = jnp.where(lane == 0, 0.0, pltpu.roll(wide, 1, 1)).astype(BF)
    dst[slot, row, 1] = block
    dst[slot, row, 2] = jnp.where(lane == 127, 0.0, pltpu.roll(wide, 127, 1)).astype(BF)


def rim(dst, planes):
    zero = jnp.zeros((3, 64, 128), BF)
    for slot in range(planes):
        dst[slot, 0] = zero
        dst[slot, 9] = zero


def window(src, plane, row):
    flat = src[pl.ds(plane, 3), pl.ds(row, 3)].reshape(1728, 128)
    return jnp.concatenate([flat, jnp.zeros((64, 128), BF)], axis=0)


def data_kernel(core, w, own, other, out, planes):
    j = core[0]
    rim(planes, 4)

    def fill(row, _):
        for s in range(3):
            put(planes, s + j, row + 1, own[:, s, row].reshape(64, 128))
        put(planes, 3 * (1 - j), row + 1, other[:, j, row].reshape(64, 128))
        return 0

    lax.fori_loop(0, 8, fill, 0)
    low = lane_half((64, 128))
    row_id = lax.broadcasted_iota(jnp.int32, (64, 128), 0)
    lane_id = lax.broadcasted_iota(jnp.int32, (64, 128), 1)
    pick = jnp.where((lane_id & 63) == row_id, 1.0, 0.0).astype(BF)
    tiles = []
    for r in range(14):
        even = w[:, 13 - r].reshape(64, 128)
        first = jnp.where(low, even.astype(F32), 0.0).astype(BF)
        if r < 13:
            odd = w[:, 12 - r].reshape(64, 128)
            second = jnp.where(low, 0.0, odd.astype(F32)).astype(BF)
        else:
            second = jnp.zeros((64, 128), BF)
        both = jnp.concatenate([first, second], axis=0)
        tiles.append(
            lax.dot_general(
                pick, both, (((1,), (1,)), ((), ())), preferred_element_type=F32
            ).astype(BF)
        )
    lhs = jnp.concatenate(tiles, axis=1)

    def row_pair(step, _):
        p, h = step // 4, 2 * (step % 4)
        rhs = jnp.concatenate([window(planes, p, h), window(planes, p, h + 1)], axis=1)
        res = jnp.dot(lhs, rhs, preferred_element_type=F32)
        out[:, p, h] = res[:, :128].reshape(4, 16, 128)
        out[:, p, h + 1] = res[:, 128:].reshape(4, 16, 128)
        return 0

    lax.fori_loop(0, 8, row_pair, 0)


def volume_kernel(core, w, vown, vother, cown, cother, out, planes, cot, acc):
    j = core[0]
    rim(planes, 6)

    def fill(row, _):
        for s in range(3):
            put(planes, 3 * j + s, row + 1, vown[:, s, row].reshape(64, 128))
            put(planes, 3 * (1 - j) + s, row + 1, vother[:, s, row].reshape(64, 128))
        for s in range(2):
            cot[2 * j + s, row] = cown[:, s + 1 - j, row].reshape(64, 128)
            cot[2 * (1 - j) + s, row] = cother[:, s, row].reshape(64, 128)
        return 0

    lax.fori_loop(0, 8, fill, 0)
    lhs = jnp.concatenate([w[:, r].reshape(64, 128) for r in range(14)], axis=1)

    def row_pair(step, _):
        p, h = step // 4, 2 * (step % 4)
        q = 2 * j + p
        rhs = jnp.concatenate([window(planes, q, h), window(planes, q, h + 1)], axis=1)
        res = jnp.dot(lhs, rhs, preferred_element_type=F32)
        at = (p * 8 + h) * 16
        out[:, pl.ds(at, 16)] = res[:, :128].reshape(4, 16, 128)
        out[:, pl.ds(at + 16, 16)] = res[:, 128:].reshape(4, 16, 128)
        return 0

    lax.fori_loop(0, 8, row_pair, 0)
    acc[...] = jnp.zeros_like(acc)
    half = pl.ds(32 * j, 32)

    def taps(p, h):
        flat = planes[pl.ds(p, 3), pl.ds(h, 3), :, half].reshape(864, 128)
        return jnp.concatenate([flat, jnp.zeros((32, 128), BF)], axis=0)

    def correlate(step, _):
        p, h = step // 4, 2 * (step % 4)
        grad = jnp.concatenate([cot[p, h], cot[p, h + 1]], axis=1)
        rhs = jnp.concatenate([taps(p, h), taps(p, h + 1)], axis=1)
        acc[...] += lax.dot_general(
            grad, rhs, (((1,), (1,)), ((), ())), preferred_element_type=F32
        )
        return 0

    lax.fori_loop(0, 16, correlate, 0)
    for g in range(7):
        out[:, 256 + 16 * g : 272 + 16 * g] = acc[:, 128 * g : 128 * g + 128].reshape(4, 16, 128)
    out[:, 368:384] = jnp.zeros((4, 16, 128), F32)


def place_kernel(core, own, other, out):
    j = core[0]
    lane = lax.broadcasted_iota(jnp.int32, (16, 128), 1) // 32
    for g in range(7):
        blocks = []
        for a in range(4):
            mine = own[a, g].astype(F32)
            theirs = other[a, g].astype(F32)
            blocks.append(jnp.where(j == 0, mine, theirs))
            blocks.append(jnp.where(j == 0, theirs, mine))
        for s in range(4):
            if 4 * g + s >= 27:
                continue
            for side in range(2):
                total = jnp.zeros((16, 128), F32)
                for at in range(4):
                    block = blocks[4 * side + at]
                    turn = (32 * (at - s)) % 128
                    block = pltpu.roll(block, turn, 1) if turn else block
                    total = jnp.where(lane == at, block, total)
                out[4 * g + s, :, 128 * side : 128 * side + 128] = total.astype(BF)


def local(volume, filters, cotangent):
    depth, height, width = volume.shape[1:]
    cells = depth * height * width * lax.axis_size("xz") * lax.axis_size("co")
    core = lax.axis_index("co")
    core_ref = core.reshape(1).astype(jnp.int32)
    chips = lax.axis_size("xz")

    fields = jnp.transpose(jnp.stack([volume, cotangent]), (0, 2, 3, 1, 4))
    outer = jnp.where(core == 0, fields[:, 0], fields[:, 1])
    links = [(2 * i + 1, 2 * i + 2) for i in range(chips - 1)]
    links = links + [(t, s) for s, t in links]
    rims = lax.ppermute(outer, ("xz", "co"), links)[:, None]
    fields = jnp.where(
        core == 0,
        jnp.concatenate([rims, fields], axis=1),
        jnp.concatenate([fields, rims], axis=1),
    )

    packed = call(pack_kernel, jax.ShapeDtypeStruct((4, 14, 16, 128), BF), [VMEM])(
        jnp.transpose(filters, (1, 2, 3, 0, 4)).reshape(27, 16, 256)
    )
    to_a = jnp.concatenate(
        [
            jnp.broadcast_to(fields[1].reshape(1, 384, 128), (4, 384, 128)),
            packed.reshape(4, 224, 128),
        ],
        axis=1,
    )
    from_a = lax.all_to_all(to_a, "a", 0, 0)
    grad = from_a[:, :384].reshape(4, 3, 8, 16, 128)
    weights = from_a[:, 384:].reshape(4, 14, 16, 128)
    vol = lax.all_to_all(jnp.broadcast_to(fields[:1], (4, 3, 8, 16, 128)), "b", 0, 0)

    swap = [(0, 1), (1, 0)]
    grad_own = jnp.where(core == 0, grad[:, 1:], grad[:, :2])
    grad_other = lax.ppermute(grad_own, "co", swap)
    vol_other = lax.ppermute(vol, "co", swap)

    data = call(
        data_kernel,
        jax.ShapeDtypeStruct((4, 2, 8, 16, 128), F32),
        [SMEM, VMEM, VMEM, VMEM],
        [pltpu.VMEM((4, 10, 3, 64, 128), BF)],
    )(core_ref, weights, grad, grad_other)
    parts = call(
        volume_kernel,
        jax.ShapeDtypeStruct((4, 384, 128), F32),
        [SMEM, VMEM, VMEM, VMEM, VMEM, VMEM],
        [
            pltpu.VMEM((6, 10, 3, 64, 128), BF),
            pltpu.VMEM((4, 8, 64, 128), BF),
            pltpu.VMEM((64, 896), F32),
        ],
    )(core_ref, weights, vol, vol_other, grad, grad_other)

    parts = lax.all_to_all(parts, "a", 0, 0)
    data = lax.all_to_all(data, "b", 0, 0)
    response = jnp.sum(parts[:, :256].reshape(4, 2, 8, 16, 128), axis=0)
    kernel = lax.all_to_all(parts[:, 256:].reshape(16, 32, 128), "xz", 0, 0)
    factor = 1.0 / math.sqrt(cells)
    kernel = (jnp.sum(kernel, axis=0) * factor).astype(BF)
    kernel = lax.all_to_all(jnp.broadcast_to(kernel[None], (16, 32, 128)), "xz", 0, 0)
    kernel = kernel.reshape(4, 8, 16, 128)
    kernel_other = lax.ppermute(kernel, "co", swap)
    placed = call(place_kernel, jax.ShapeDtypeStruct((27, 16, 256), BF), [SMEM, VMEM, VMEM])(
        core_ref, kernel, kernel_other
    )
    order = (2, 0, 1, 3)
    return (
        jnp.transpose(response.astype(BF), order),
        jnp.transpose(jnp.sum(data, axis=0).astype(BF), order),
        jnp.transpose(placed.reshape(3, 3, 3, 16, 256), (3, 0, 1, 2, 4)),
    )


def solution(mesh):
    grid = Mesh(mesh.devices.reshape(16, 2, 4, 4), ("xz", "co", "a", "b"))
    cells = P(("a", "b"), ("xz", "co"), None, None)
    kernel = P(("a", "b"), None, None, None, None)
    return jax.shard_map(
        local,
        mesh=grid,
        in_specs=(cells, kernel, cells),
        out_specs=(cells, cells, kernel),
        check_vma=False,
    )
```

time: 525 us -> 150 us (0.29)
  waiting for transfers between devices: 434 us -> 51.4 us
  local copies, waits for them, and re-layouts: 32.7 us -> 4.54 us
  starting transfers between devices: 28.2 us -> 55.7 us
  blocking collectives: 0 us -> 22.5 us
  Pallas kernels: 0 us -> 13.4 us
  between operations: 14.2 us -> 0.81 us
  matrix products: 7.03 us -> 0 us
  other arithmetic: 7.52 us -> 1.05 us
    psum x1 -> x0, waiting for transfers between devices: 263 us -> none  [local(): kernel_total = lax.psum(kernel_part, 'sp')]
    all_gather x2 -> x0, waiting for transfers between devices: 153 us -> none  [the longest x1 96.8 us: local(): lax.all_gather(rimmed, 'ch', axis=0, tiled=True)]
    all_to_all x1 -> x5, waiting for transfers between devices: 14.2 us -> 47.8 us  [the longest x1 15.8 us: local(): data = lax.all_to_all(data, 'b', 0, 0)]
    all_to_all x1 -> x5, starting transfers between devices: 13.7 us -> 41.5 us  [the longest x1 13.4 us: local(): kernel = lax.all_to_all(parts[:, 256:].reshape(16, 32, 128), 'xz', 0, 0)]
    all_to_all x0 -> x1, blocking collectives: none -> 22.5 us  [local(): parts = lax.all_to_all(parts, 'a', 0, 0)]
    pallas_call x0 -> x4, Pallas kernels: none -> 13.4 us  [the longest x1 7.89 us: local(): call(volume_kernel, jax.ShapeDtypeStruct((4, 384, 128), F32), [SMEM, VMEM...]
    unnamed x41 -> x4, local copies, waits for them, and re-layouts: 12 us -> 1.3 us
    reshape x6 -> x0, local copies, waits for them, and re-layouts: 7.61 us -> none  [the longest x3 3.83 us: forward_terms(): rows = piece[:, depth_tap:depth_tap + depth].reshape(count, -1)]
  transfers between devices with their start and end apart: 8 -> 9, of which waited for: 6 -> 8; matrix products, arithmetic and copies ran while one was open for 5% -> 2% of each run, Pallas kernels for 0% -> 3%
where the time goes in v1:
time: 150 us; the launch traced here: 149 us
  starting transfers between devices  55.7 us (37%)
  waiting for transfers between devices  51.4 us (34%)
  blocking collectives  22.5 us (15%)
  Pallas kernels  13.4 us (9%)
  local copies, waits for them, and re-layouts  4.54 us (3%)
    all_to_all x1, blocking collectives, local(): parts = lax.all_to_all(parts, 'a', 0, 0)  22.5 us
    all_to_all x1, waiting for transfers between devices, local(): data = lax.all_to_all(data, 'b', 0, 0)  15.8 us
    all_to_all x1, starting transfers between devices, local(): kernel = lax.all_to_all(parts[:, 256:].reshape(16, 32, 128), 'xz', 0, 0)  13.4 us
    all_to_all x1, waiting for transfers between devices, local(): lax.all_to_all(jnp.broadcast_to(fields[:1], (4, 3, 8, 16, 128)), 'b', 0, 0)  11.8 us
    all_to_all x1, starting transfers between devices, local(): lax.all_to_all(jnp.broadcast_to(fields[:1], (4, 3, 8, 16, 128)), 'b', 0, 0)  10.1 us
    all_to_all x1, waiting for transfers between devices, local(): from_a = lax.all_to_all(to_a, 'a', 0, 0)  10.1 us
    pallas_call x1, Pallas kernels, local(): call(volume_kernel, jax.ShapeDtypeStruct((4, 384, 128), F32), [SMEM, VMEM...  7.89 us
    all_to_all x1, starting transfers between devices, local(): data = lax.all_to_all(data, 'b', 0, 0)  7.77 us
  transfers between devices with their start and end apart: 9, of which 8 were waited for; matrix products, arithmetic and copies ran while one was open for 2% of the time, Pallas kernels for 3%

profile of v1, /device:TPU:1, one launch (start us, length us, event | category | flops | bytes accessed | tf_op | source)
XLA Modules:
  0.0 149.4 jit_solution(17362295966998557496)
XLA Ops:
  0.6 0.9 copy_bitcast_fusion
  1.6 5.4 %collective-permute-start = (bf16[2,8,16,128]{3,2,1,0:T(8,128)(2,1)S(1)}, bf16[2,8,16,128]{3,2,1,0:T(8,128)(2,1)S(1)}, u32[]{:S(2)}, u32[]{:S(2)}) collective-permute-start(bf16[2,8,16,128]{3,2,1,0:T(8,128)(2,1)S(1)} %fusion), channel_id=1, source_target_pairs={{16,32},{48,64},{80,96},{112,128},{144,160},{176,192},{208,224},{2... | collective-permute-start | bytes 196616 | tf_op jit(solution)/shard_map/ppermute | solution.py:195
  7.0 1.9 %collective-permute-done = bf16[2,8,16,128]{3,2,1,0:T(8,128)(2,1)S(1)} collective-permute-done((bf16[2,8,16,128]{3,2,1,0:T(8,128)(2,1)S(1)}, bf16[2,8,16,128]{3,2,1,0:T(8,128)(2,1)S(1)}, u32[]{:S(2)}, u32[]{:S(2)}) %collective-permute-start) | collective-permute-done | bytes 65568 | tf_op jit(solution)/shard_map/ppermute | solution.py:195
  9.0 0.0 copy-start
  9.0 0.8 broadcast_in_dim.27
  9.8 10.1 %all-to-all-start.1 = ((bf16[4,3,8,16,128]{4,3,2,1,0:T(8,128)(2,1)}), bf16[4,3,8,16,128]{4,3,2,1,0:T(8,128)(2,1)S(1)}, u32[]{:S(2)}, u32[]{:S(2)}) async-start(bf16[4,3,8,16,128]{4,3,2,1,0:T(8,128)(2,1)} %broadcast_in_dim.27), calls=%async_computation.1 | async-start | bytes 786432 | tf_op jit(solution)/shard_map/all_to_all | solution.py:215
  19.9 0.0 copy-done
  19.9 0.1 shard_map.58
  20.1 0.1 broadcast_in_dim.25
  20.1 0.9 pad_maximum_fusion
  21.0 11.8 %all-to-all-done.1.vown = bf16[4,3,8,16,128]{4,3,2,1,0:T(8,128)(2,1)S(1)} async-done(((bf16[4,3,8,16,128]{4,3,2,1,0:T(8,128)(2,1)}), bf16[4,3,8,16,128]{4,3,2,1,0:T(8,128)(2,1)S(1)}, u32[]{:S(2)}, u32[]{:S(2)}) %all-to-all-start.1) | async-done | bytes 393248 | tf_op jit(solution)/shard_map/all_to_all | solution.py:215
  32.8 5.9 %all-to-all-start = ((bf16[4,608,128]{2,1,0:T(8,128)(2,1)}), bf16[4,608,128]{2,1,0:T(8,128)(2,1)S(1)}, u32[]{:S(2)}, u32[]{:S(2)}) async-start(bf16[4,608,128]{2,1,0:T(8,128)(2,1)} %pad_maximum_fusion), calls=%async_computation | async-start | bytes 1245184 | tf_op jit(solution)/shard_map/all_to_all | solution.py:212
  38.7 1.9 %collective-permute-start.1 = (bf16[4,3,8,16,128]{4,3,2,1,0:T(8,128)(2,1)S(1)}, bf16[4,3,8,16,128]{4,3,2,1,0:T(8,128)(2,1)S(1)}, u32[]{:S(2)}, u32[]{:S(2)}) collective-permute-start(bf16[4,3,8,16,128]{4,3,2,1,0:T(8,128)(2,1)S(1)} %all-to-all-done.1.vown), channel_id=1, source_target_pairs={{0,16},{16,0},{1,17},{17,1},{2,18},{18,2},{3,19},{19,3},{4,20},{20... | collective-permute-start | bytes 1179656 | tf_op jit(solution)/shard_map/ppermute | solution.py:220
  40.6 10.1 %all-to-all-done = bf16[4,608,128]{2,1,0:T(8,128)(2,1)S(1)} async-done(((bf16[4,608,128]{2,1,0:T(8,128)(2,1)}), bf16[4,608,128]{2,1,0:T(8,128)(2,1)S(1)}, u32[]{:S(2)}, u32[]{:S(2)}) %all-to-all-start) | async-done | bytes 622624 | tf_op jit(solution)/shard_map/all_to_all | solution.py:212
  50.8 1.9 %collective-permute-start.2 = (bf16[4,2,8,16,128]{4,3,2,1,0:T(8,128)(2,1)S(1)}, bf16[4,2,8,16,128]{4,3,2,1,0:T(8,128)(2,1)S(1)}, u32[]{:S(2)}, u32[]{:S(2)}) collective-permute-start(bf16[4,2,8,16,128]{4,3,2,1,0:T(8,128)(2,1)S(1)} %slice_select_fusion), channel_id=1, source_target_pairs={{0,16},{16,0},{1,17},{17,1},{2,18},{18,2},{3,19},{19,3},{4,20},{20... | collective-permute-start | bytes 786440 | tf_op jit(solution)/shard_map/ppermute | solution.py:219
  52.7 0.0 collective-permute-done.1.vother
  52.7 1.5 collective-permute-done.2.cother.other
  54.2 7.9 %shard_map.59 = f32[4,384,128]{2,1,0:T(8,128)S(1)} custom-call(s32[1]{0:T(128)} %bitcast.core, bf16[4,14,16,128]{3,2,1,0:T(8,128)(2,1)S(1)} %bitcast.35, bf16[4,3,8,16,128]{4,3,2,1,0:T(8,128)(2,1)S(1)} %all-to-all-done.1.vown, bf16[4,3,8,16,128]{4,3,2,1,0:T(8,128)(2,1)S(1)} %collective-permute-done.1.vother, bf16[4,3,8,16,128]{4,3,2,1,0:T(8,128)(2,1)S(1)} %bitcast.33, ...), custom_call_target="tpu_custom_call" | custom-call | tf_op jit(solution)/shard_map/pallas_call | solution.py:228
  62.1 22.5 %all_to_all.30 = f32[4,384,128]{2,1,0:T(8,128)S(1)} all-to-all(f32[4,384,128]{2,1,0:T(8,128)S(1)} %shard_map.59), channel_id=1, replica_groups=mesh['xz'=16,'co'=2,'a'=4,'b'=4] {'a'}, dimensions={0} | all-to-all | bytes 1572864 | tf_op jit(solution)/shard_map/all_to_all | solution.py:239
  84.6 0.7 slice.49
  85.3 13.4 %all-to-all-start.4 = ((f32[16,32,128]{2,1,0:T(8,128)}), f32[16,32,128]{2,1,0:T(8,128)S(1)}, u32[]{:S(2)}, u32[]{:S(2)}) async-start(f32[16,32,128]{2,1,0:T(8,128)} %bitcast.17), calls=%async_computation.4 | async-start | bytes 524288 | tf_op jit(solution)/shard_map/all_to_all | solution.py:242
  98.7 4.4 %shard_map.60 = f32[4,2,8,16,128]{4,3,2,1,0:T(8,128)} custom-call(s32[1]{0:T(128)} %bitcast.core, bf16[4,14,16,128]{3,2,1,0:T(8,128)(2,1)S(1)} %bitcast.36, bf16[4,3,8,16,128]{4,3,2,1,0:T(8,128)(2,1)S(1)} %bitcast.34, bf16[4,2,8,16,128]{4,3,2,1,0:T(8,128)(2,1)S(1)} %collective-permute-done.2.cother.other), custom_call_target="tpu_custom_call" | custom-call | tf_op jit(solution)/shard_map/pallas_call | solution.py:222
  103.1 3.6 %all-to-all-done.4 = f32[16,32,128]{2,1,0:T(8,128)S(1)} async-done(((f32[16,32,128]{2,1,0:T(8,128)}), f32[16,32,128]{2,1,0:T(8,128)S(1)}, u32[]{:S(2)}, u32[]{:S(2)}) %all-to-all-start.4) | async-done | bytes 262176 | tf_op jit(solution)/shard_map/all_to_all | solution.py:242
  106.7 7.8 %all-to-all-start.3 = ((f32[4,2,8,16,128]{4,3,2,1,0:T(8,128)}), f32[4,2,8,16,128]{4,3,2,1,0:T(8,128)S(1)}, u32[]{:S(2)}, u32[]{:S(2)}) async-start(f32[4,2,8,16,128]{4,3,2,1,0:T(8,128)} %shard_map.60), calls=%async_computation.3 | async-start | bytes 1048576 | tf_op jit(solution)/shard_map/all_to_all | solution.py:240
  114.5 15.8 %all-to-all-done.3 = f32[4,2,8,16,128]{4,3,2,1,0:T(8,128)S(1)} async-done(((f32[4,2,8,16,128]{4,3,2,1,0:T(8,128)}), f32[4,2,8,16,128]{4,3,2,1,0:T(8,128)S(1)}, u32[]{:S(2)}, u32[]{:S(2)}) %all-to-all-start.3) | async-done | bytes 524320 | tf_op jit(solution)/shard_map/all_to_all | solution.py:240
  130.3 0.7 broadcast_in_dim.28
  130.9 4.3 %all-to-all-start.5 = ((bf16[16,32,128]{2,1,0:T(8,128)(2,1)}), bf16[16,32,128]{2,1,0:T(8,128)(2,1)S(1)}, u32[]{:S(2)}, u32[]{:S(2)}) async-start(bf16[16,32,128]{2,1,0:T(8,128)(2,1)} %broadcast_in_dim.28), calls=%async_computation.5 | async-start | bytes 262144 | tf_op jit(solution)/shard_map/all_to_all | solution.py:245
  135.3 0.6 copy.21
  136.0 6.6 %all-to-all-done.5 = bf16[16,32,128]{2,1,0:T(8,128)(2,1)S(1)} async-done(((bf16[16,32,128]{2,1,0:T(8,128)(2,1)}), bf16[16,32,128]{2,1,0:T(8,128)(2,1)S(1)}, u32[]{:S(2)}, u32[]{:S(2)}) %all-to-all-start.5) | async-done | bytes 131104 | tf_op jit(solution)/shard_map/all_to_all | solution.py:245
  142.5 4.9 %collective-permute-start.3 = (bf16[4,8,16,128]{3,2,1,0:T(8,128)(2,1)S(1)}, bf16[4,8,16,128]{3,2,1,0:T(8,128)(2,1)S(1)}, u32[]{:S(2)}, u32[]{:S(2)}) collective-permute-start(bf16[4,8,16,128]{3,2,1,0:T(8,128)(2,1)S(1)} %bitcast.38), channel_id=1, source_target_pairs={{0,16},{16,0},{1,17},{17,1},{2,18},{18,2},{3,19},{19,3},{4,20},{20... | collective-permute-start | bytes 393224 | tf_op jit(solution)/shard_map/ppermute | solution.py:247
  147.5 0.6 copy.20
  148.1 0.3 collective-permute-done.3.other
  148.4 0.9 shard_map.61
  (11 shorter events, 0.2 us)
Async XLA Ops:
  1.6 7.3 %collective-permute-start = (bf16[2,8,16,128]{3,2,1,0:T(8,128)(2,1)S(1)}, bf16[2,8,16,128]{3,2,1,0:T(8,128)(2,1)S(1)}, u32[]{:S(2)}, u32[]{:S(2)}) collective-permute-start(bf16[2,8,16,128]{3,2,1,0:T(8,128)(2,1)S(1)} %fusion), channel_id=1, source_target_pairs={{16,32},{48,64},{80,96},{112,128},{144,160},{176,192},{208,224},{2... | collective-permute-start | bytes 196616 | tf_op jit(solution)/shard_map/ppermute | solution.py:195
  9.0 11.0 %copy-start = (bf16[16,3,3,3,256]{4,0,3,2,1:T(8,128)(2,1)S(1)}, bf16[16,3,3,3,256]{4,0,3,2,1:T(8,128)(2,1)}, u32[]{:S(2)}) copy-start(bf16[16,3,3,3,256]{4,0,3,2,1:T(8,128)(2,1)} %param.4) | copy-start | bytes 663556
  9.8 23.0 %all-to-all-start.1 = ((bf16[4,3,8,16,128]{4,3,2,1,0:T(8,128)(2,1)}), bf16[4,3,8,16,128]{4,3,2,1,0:T(8,128)(2,1)S(1)}, u32[]{:S(2)}, u32[]{:S(2)}) async-start(bf16[4,3,8,16,128]{4,3,2,1,0:T(8,128)(2,1)} %broadcast_in_dim.27), calls=%async_computation.1 | async-start | bytes 786432 | tf_op jit(solution)/shard_map/all_to_all | solution.py:215
  32.8 17.9 %all-to-all-start = ((bf16[4,608,128]{2,1,0:T(8,128)(2,1)}), bf16[4,608,128]{2,1,0:T(8,128)(2,1)S(1)}, u32[]{:S(2)}, u32[]{:S(2)}) async-start(bf16[4,608,128]{2,1,0:T(8,128)(2,1)} %pad_maximum_fusion), calls=%async_computation | async-start | bytes 1245184 | tf_op jit(solution)/shard_map/all_to_all | solution.py:212
  38.7 14.0 %collective-permute-start.1 = (bf16[4,3,8,16,128]{4,3,2,1,0:T(8,128)(2,1)S(1)}, bf16[4,3,8,16,128]{4,3,2,1,0:T(8,128)(2,1)S(1)}, u32[]{:S(2)}, u32[]{:S(2)}) collective-permute-start(bf16[4,3,8,16,128]{4,3,2,1,0:T(8,128)(2,1)S(1)} %all-to-all-done.1.vown), channel_id=1, source_target_pairs={{0,16},{16,0},{1,17},{17,1},{2,18},{18,2},{3,19},{19,3},{4,20},{20... | collective-permute-start | bytes 1179656 | tf_op jit(solution)/shard_map/ppermute | solution.py:220
  50.8 3.4 %collective-permute-start.2 = (bf16[4,2,8,16,128]{4,3,2,1,0:T(8,128)(2,1)S(1)}, bf16[4,2,8,16,128]{4,3,2,1,0:T(8,128)(2,1)S(1)}, u32[]{:S(2)}, u32[]{:S(2)}) collective-permute-start(bf16[4,2,8,16,128]{4,3,2,1,0:T(8,128)(2,1)S(1)} %slice_select_fusion), channel_id=1, source_target_pairs={{0,16},{16,0},{1,17},{17,1},{2,18},{18,2},{3,19},{19,3},{4,20},{20... | collective-permute-start | bytes 786440 | tf_op jit(solution)/shard_map/ppermute | solution.py:219
  85.3 21.4 %all-to-all-start.4 = ((f32[16,32,128]{2,1,0:T(8,128)}), f32[16,32,128]{2,1,0:T(8,128)S(1)}, u32[]{:S(2)}, u32[]{:S(2)}) async-start(f32[16,32,128]{2,1,0:T(8,128)} %bitcast.17), calls=%async_computation.4 | async-start | bytes 524288 | tf_op jit(solution)/shard_map/all_to_all | solution.py:242
  106.7 23.6 %all-to-all-start.3 = ((f32[4,2,8,16,128]{4,3,2,1,0:T(8,128)}), f32[4,2,8,16,128]{4,3,2,1,0:T(8,128)S(1)}, u32[]{:S(2)}, u32[]{:S(2)}) async-start(f32[4,2,8,16,128]{4,3,2,1,0:T(8,128)} %shard_map.60), calls=%async_computation.3 | async-start | bytes 1048576 | tf_op jit(solution)/shard_map/all_to_all | solution.py:240
  130.9 11.6 %all-to-all-start.5 = ((bf16[16,32,128]{2,1,0:T(8,128)(2,1)}), bf16[16,32,128]{2,1,0:T(8,128)(2,1)S(1)}, u32[]{:S(2)}, u32[]{:S(2)}) async-start(bf16[16,32,128]{2,1,0:T(8,128)(2,1)} %broadcast_in_dim.28), calls=%async_computation.5 | async-start | bytes 262144 | tf_op jit(solution)/shard_map/all_to_all | solution.py:245
  142.5 5.9 %collective-permute-start.3 = (bf16[4,8,16,128]{3,2,1,0:T(8,128)(2,1)S(1)}, bf16[4,8,16,128]{3,2,1,0:T(8,128)(2,1)S(1)}, u32[]{:S(2)}, u32[]{:S(2)}) collective-permute-start(bf16[4,8,16,128]{3,2,1,0:T(8,128)(2,1)S(1)} %bitcast.38), channel_id=1, source_target_pairs={{0,16},{16,0},{1,17},{17,1},{2,18},{18,2},{3,19},{19,3},{4,20},{20... | collective-permute-start | bytes 393224 | tf_op jit(solution)/shard_map/ppermute | solution.py:247

commit v2 on v0

v2 whole, which is shorter than its diff:
```python
import math

import jax
import jax.numpy as jnp
from jax import lax
from jax.experimental import pallas as pl
from jax.experimental.pallas import tpu as pltpu
from jax.sharding import Mesh
from jax.sharding import PartitionSpec as P

BF = jnp.bfloat16
F32 = jnp.float32
F16 = jnp.float16
VMEM = pl.BlockSpec(memory_space=pltpu.VMEM)
SMEM = pl.BlockSpec(memory_space=pltpu.SMEM)
PARAMS = pltpu.CompilerParams(vmem_limit_bytes=48 * 1024 * 1024)
NT = (((1,), (1,)), ((), ()))


def call(kernel, out_shape, operands, scratch=(), micros=1):
    return pl.pallas_call(
        kernel,
        out_shape=out_shape,
        in_specs=[SMEM] + [VMEM] * (len(operands) - 1),
        out_specs=jax.tree.map(lambda _: VMEM, out_shape),
        scratch_shapes=list(scratch),
        compiler_params=PARAMS,
        cost_estimate=pl.CostEstimate(
            flops=int(micros * 1e9), bytes_accessed=1 << 18, transcendentals=0
        ),
    )(*operands)


def iota(shape, dim):
    return lax.broadcasted_iota(jnp.int32, shape, dim)


def size_of(peak):
    most = jnp.max(jnp.max(peak, axis=0, keepdims=True), axis=1, keepdims=True)
    power = jnp.floor(jnp.log2(jnp.clip(most, 2.0**-100, 2.0**100)))
    return jnp.broadcast_to(power, (8, 128))


def pack_kernel(place, fil, own, send):
    zh = place[2]
    lane = iota((256, 256), 1)
    wanted = (lane % 128) // 16 * 32 + (zh ^ (lane // 128)) * 16 + lane % 16
    pick = jnp.where(iota((256, 256), 0) == wanted, 1.0, 0.0).astype(BF)
    res = jnp.dot(fil[...].reshape(432, 256), pick, preferred_element_type=F32).astype(BF)
    own[...] = res[:, :128].reshape(27, 16, 128)
    send[...] = res[:, 128:].reshape(27, 16, 128)


def put(dst, slot, row, block):
    wide = block.astype(F32)
    lane = iota(block.shape, 1)
    dst[slot, row, 0] = jnp.where(lane == 0, 0.0, pltpu.roll(wide, 1, 1)).astype(BF)
    dst[slot, row, 1] = block
    dst[slot, row, 2] = jnp.where(lane == 127, 0.0, pltpu.roll(wide, 127, 1)).astype(BF)


def data_kernel(place, wown, wgot, own, got, other, rim, out, power, planes, peak):
    j = place[0]
    zero = jnp.zeros((3, 32, 128), BF)
    for slot in range(4):
        planes[slot, 0] = zero
        planes[slot, 9] = zero

    def fill(row, _):
        for s in range(2):
            put(planes, 1 + s, row + 1, jnp.concatenate([own[s, row], got[s, row]], axis=0))
        near = jnp.concatenate([other[0, j, row], other[1, j, row]], axis=0)
        put(planes, 3 * (1 - j), row + 1, near)
        put(planes, 3 * j, row + 1, jnp.concatenate([rim[0, row], rim[1, row]], axis=0))
        return 0

    lax.fori_loop(0, 8, fill, 0)
    peak[...] = jnp.zeros_like(peak)
    same = jnp.where(iota((128, 128), 0) == iota((128, 128), 1), 1.0, 0.0).astype(BF)
    tiles = []
    for g in range(7):
        rows = []
        for s in range(4):
            t = 26 - 4 * g - s
            rows += [wown[t], wgot[t]] if t >= 0 else [jnp.zeros((32, 128), BF)]
        tile = lax.dot_general(
            same, jnp.concatenate(rows, axis=0), NT, preferred_element_type=F32
        )
        tiles.append(tile.astype(BF))
    lhs = jnp.concatenate(tiles, axis=1)

    def window(plane, row):
        flat = planes[pl.ds(plane, 3), pl.ds(row, 3)].reshape(864, 128)
        return jnp.concatenate([flat, jnp.zeros((32, 128), BF)], axis=0)

    def row_pair(step, _):
        p, h = step // 4, 2 * (step % 4)
        rhs = jnp.concatenate([window(p, h), window(p, h + 1)], axis=1)
        res = jnp.dot(lhs, rhs, preferred_element_type=F32)
        at = (p * 8 + h) * 16
        out[:, pl.ds(at, 16)] = res[:, :128].reshape(8, 16, 128)
        out[:, pl.ds(at + 16, 16)] = res[:, 128:].reshape(8, 16, 128)
        sizes = jnp.maximum(jnp.abs(res[:, :128]), jnp.abs(res[:, 128:]))
        peak[...] = jnp.maximum(peak[...], jnp.max(sizes.reshape(16, 8, 128), axis=0))
        return 0

    lax.fori_loop(0, 8, row_pair, 0)
    size = size_of(peak[...])
    power[:8] = size
    power[8:] = size


def volume_kernel(
    place, wown, wgot, vown, vother, cown, cgot, cother, keep, send, power, planes, cot, resp, acc
):
    j = place[0]
    cot[...] = jnp.zeros_like(cot)
    resp[...] = jnp.zeros_like(resp)
    half = pl.ds(pl.multiple_of(64 * j, 64), 64)

    def fill(row, _):
        for s in range(3):
            put(planes, 3 * j + s, row, vown[:, s, row].reshape(128, 128))
            put(planes, 3 * (1 - j) + s, row, vother[:, s, row].reshape(128, 128))
        for s in range(2):
            cot[2 + 2 * j + s, row + 1] = jnp.concatenate([cown[s, row], cgot[s, row]], axis=0)
            cot[4 - 2 * j + s, row + 1] = jnp.concatenate(
                [cother[0, s, row], cother[1, s, row]], axis=0
            )
        return 0

    lax.fori_loop(0, 8, fill, 0)

    weights = jnp.concatenate(
        [
            jnp.concatenate(
                [jnp.concatenate([wown[3 * ab + c], wgot[3 * ab + c]], axis=0) for c in range(3)],
                axis=1,
            )
            for ab in range(9)
        ],
        axis=0,
    )

    def row_pair(step, _):
        h = 2 * step
        for q in range(4):
            taps = [a for a in range(3) if 0 <= q - a < 2]
            lhs = weights[96 * taps[0] : 96 * taps[-1] + 96]
            first = planes[2 * j + q, h].reshape(384, 128)
            second = planes[2 * j + q, h + 1].reshape(384, 128)
            res = jnp.dot(
                lhs, jnp.concatenate([first, second], axis=1), preferred_element_type=F32
            )
            for n, a in enumerate(taps):
                for b in range(3):
                    at = 96 * n + 32 * b
                    resp[q - a, h + 2 - b] += res[at : at + 32, :128]
                    resp[q - a, h + 3 - b] += res[at : at + 32, 128:]
        return 0

    lax.fori_loop(0, 4, row_pair, 0)
    peak = jnp.zeros((8, 128), F32)
    for p in range(2):
        for h in range(8):
            at = (p * 8 + h) * 16
            keep[at : at + 16] = resp[p, h + 1, :16]
            part = resp[p, h + 1, 16:]
            send[at : at + 16] = part
            peak = jnp.maximum(peak, jnp.max(jnp.abs(part).reshape(2, 8, 128), axis=0))
    power[:8] = size_of(peak)

    acc[...] = jnp.zeros_like(acc)
    for q in range(6):
        low, high = max(0, 2 - q), min(2, 5 - q)
        lhs, rhs = [], []
        for h in range(8):
            grads = cot[q + low : q + high + 1, h : h + 3]
            lhs.append(grads.reshape(96 * (high - low + 1), 128))
            taps = planes[q, h, :, half].reshape(192, 128)
            rhs.append(jnp.concatenate([taps, jnp.zeros((64, 128), BF)], axis=0))
        res = lax.dot_general(
            jnp.concatenate(lhs, axis=1),
            jnp.concatenate(rhs, axis=1),
            NT,
            preferred_element_type=F32,
        )
        acc[96 * low : 96 * high + 96] += res
    for side, out in enumerate((keep, send)):
        third = []
        for ab in range(9):
            rows = pl.ds(32 * ab + 16 * side, 16)
            out[256 + 16 * ab : 272 + 16 * ab] = acc[rows, :128]
            third.append(acc[rows, 128:])
        for n in range(5):
            tile = third[2 * n]
            if n < 4:
                tile = tile + pltpu.roll(third[2 * n + 1], 64, 1)
            out[400 + 16 * n : 416 + 16 * n] = tile
        out[480:512] = jnp.zeros((32, 128), F32)
    peak = jnp.max(jnp.abs(send[256:480]).reshape(28, 8, 128), axis=0)
    power[8:] = size_of(peak)


def place_kernel(place, own, other, out):
    j, zh = place[0], place[2]
    lane, n = iota((128, 512), 0), iota((128, 512), 1)
    y, z, i, s = n % 256 // 32, n % 32 // 16, n % 16, n // 256
    source = s * 64 + y % 4 * 16 + i
    total = jnp.zeros((224, 512), F32)
    for core, ref in enumerate((own, other)):
        for turn in range(2):
            hit = (lane == source) & (y // 4 == (j ^ core)) & ((z ^ zh) == turn)
            pick = jnp.where(hit, 1.0, 0.0).astype(BF)
            part = ref[turn, :14].reshape(224, 128)
            total = total + jnp.dot(part, pick, preferred_element_type=F32)
    for r in range(14):
        for s in range(2):
            ab, c = (r, s) if r < 9 else (2 * (r - 9) + s, 2)
            if ab > 8:
                continue
            t = (2 - ab // 3) * 9 + (2 - ab % 3) * 3 + c
            out[t] = total[16 * r : 16 * r + 16, 256 * s : 256 * s + 256].astype(BF)


def shrink(value, power):
    return (value * jnp.exp2(14.0 - power)).astype(F16)


def grow(value, power):
    return value.astype(F32) * jnp.exp2(power.astype(F32) - 14.0)


def local(volume, filters, cotangent):
    depth, height, width = volume.shape[1:]
    cells = depth * height * width * lax.axis_size("xz") * lax.axis_size("co")
    chips = lax.axis_size("xz")
    core = lax.axis_index("co")
    place = jnp.stack([core, lax.axis_index("y"), lax.axis_index("zh")]).astype(jnp.int32)
    swap = [(0, 1), (1, 0)]

    fields = jnp.transpose(jnp.stack([volume, cotangent]), (0, 2, 3, 1, 4))
    grad = fields[1]
    near = [(2 * i + 1, 2 * i + 2) for i in range(chips - 1)]
    near = near + [(t, s) for s, t in near]

    def rim_of(value, axis):
        return lax.dynamic_index_in_dim(value, core, axis, keepdims=False)

    tap_blocks = jnp.transpose(filters, (1, 2, 3, 0, 4)).reshape(27, 16, 256)
    wown, wsend = call(
        pack_kernel, [jax.ShapeDtypeStruct((27, 16, 128), BF)] * 2, [place, tap_blocks]
    )
    pair = lax.ppermute(
        jnp.concatenate([grad.reshape(256, 128), wsend.reshape(432, 128)]), "zh", swap
    )
    grad_got = pair[:256].reshape(2, 8, 16, 128)
    wgot = pair[256:].reshape(27, 16, 128)
    both = jnp.stack([grad, grad_got])
    grad_other = lax.ppermute(both, "co", swap)
    grad_rim = lax.ppermute(rim_of(both, 1), ("xz", "co"), near)

    data, size = call(
        data_kernel,
        [jax.ShapeDtypeStruct((8, 256, 128), F32), jax.ShapeDtypeStruct((16, 128), F32)],
        [place, wown, wgot, grad, grad_got, grad_other, grad_rim],
        [pltpu.VMEM((4, 10, 3, 32, 128), BF), pltpu.VMEM((8, 128), F32)],
        micros=6,
    )
    data = jnp.concatenate(
        [shrink(data, size[0, 0]), jnp.broadcast_to(size[None].astype(F16), (8, 16, 128))], axis=1
    )
    rim = lax.ppermute(rim_of(fields[0], 0), ("xz", "co"), near)[None]
    slab = jnp.where(
        core == 0,
        jnp.concatenate([rim, fields[0]], axis=0),
        jnp.concatenate([fields[0], rim], axis=0),
    )
    vol = lax.all_to_all(jnp.broadcast_to(slab[None], (8, 3, 8, 16, 128)), "y", 0, 0)
    vol, data = lax.optimization_barrier((vol, data))
    vol_other = lax.ppermute(vol, "co", swap)
    keep, send, size = call(
        volume_kernel,
        [jax.ShapeDtypeStruct((512, 128), F32)] * 2 + [jax.ShapeDtypeStruct((16, 128), F32)],
        [place, wown, wgot, vol, vol_other, grad, grad_got, grad_other],
        [
            pltpu.VMEM((6, 8, 3, 128, 128), BF),
            pltpu.VMEM((8, 10, 32, 128), BF),
            pltpu.VMEM((2, 10, 32, 128), F32),
            pltpu.VMEM((288, 256), F32),
        ],
        micros=8,
    )
    send = jnp.concatenate(
        [shrink(send[:256], size[0, 0]), shrink(send[256:], size[8, 0]), size.astype(F16)]
    )
    got = lax.ppermute(send, "zh", swap)
    data = lax.all_to_all(data, "y", 0, 0)
    keep, got, data = lax.optimization_barrier((keep, got, data))

    kernel = jnp.concatenate([keep[256:], grow(got[256:512], got[520, 0])]).reshape(16, 32, 128)
    kernel = lax.all_to_all(kernel, "xz", 0, 0)
    factor = 1.0 / math.sqrt(cells)
    kernel = (jnp.sum(kernel, axis=0) * factor).astype(BF)
    kernel = lax.all_to_all(jnp.broadcast_to(kernel[None], (16, 32, 128)), "xz", 0, 0)
    kernel = kernel.reshape(2, 16, 16, 128)
    kernel_other = lax.ppermute(kernel, "co", swap)
    placed = call(
        place_kernel, jax.ShapeDtypeStruct((27, 16, 256), BF), [place, kernel, kernel_other]
    )
    order = (2, 0, 1, 3)
    response = (keep[:256] + grow(got[:256], got[512, 0])).reshape(2, 8, 16, 128)
    data = jnp.sum(grow(data[:, :256], data[:, 256:257, :1]), axis=0).reshape(2, 8, 16, 128)
    return (
        jnp.transpose(response.astype(BF), order),
        jnp.transpose(data.astype(BF), order),
        jnp.transpose(placed.reshape(3, 3, 3, 16, 256), (3, 0, 1, 2, 4)),
    )


def solution(mesh):
    grid = Mesh(mesh.devices.reshape(16, 2, 8, 2), ("xz", "co", "y", "zh"))
    cells = P(("y", "zh"), ("xz", "co"), None, None)
    kernel = P(("y", "zh"), None, None, None, None)
    return jax.shard_map(
        local,
        mesh=grid,
        in_specs=(cells, kernel, cells),
        out_specs=(cells, cells, kernel),
        check_vma=False,
    )
```

time: 525 us -> 113 us (0.22)
  waiting for transfers between devices: 434 us -> 28.3 us
  local copies, waits for them, and re-layouts: 32.7 us -> 5.62 us
  blocking collectives: 0 us -> 18.5 us
  starting transfers between devices: 28.2 us -> 43.9 us
  Pallas kernels: 0 us -> 10.4 us
  between operations: 14.2 us -> 4.36 us
  matrix products: 7.03 us -> 0 us
  other arithmetic: 7.52 us -> 1.73 us
    psum x1 -> x0, waiting for transfers between devices: 263 us -> none  [local(): kernel_total = lax.psum(kernel_part, 'sp')]
    all_gather x2 -> x0, waiting for transfers between devices: 153 us -> none  [the longest x1 96.8 us: local(): lax.all_gather(rimmed, 'ch', axis=0, tiled=True)]
    all_to_all x0 -> x1, blocking collectives: none -> 18.5 us  [local(): kernel = lax.all_to_all(kernel, 'xz', 0, 0)]
    ppermute x4 -> x7, starting transfers between devices: 14.4 us -> 29.5 us  [the longest x1 9.73 us: local(): lax.ppermute(jnp.concatenate([grad.reshape(256, 128), wsend.reshape(432,...]
    unnamed x41 -> x3, local copies, waits for them, and re-layouts: 12 us -> 0.65 us
    pallas_call x0 -> x4, Pallas kernels: none -> 10.4 us  [call(): pl.pallas_call(kernel, out_shape=out_shape, in_specs=[SMEM] + [VMEM] * (l...]
    reshape x6 -> x0, local copies, waits for them, and re-layouts: 7.61 us -> none  [the longest x3 3.83 us: forward_terms(): rows = piece[:, depth_tap:depth_tap + depth].reshape(count, -1)]
    ppermute x4 -> x7, waiting for transfers between devices: 4.09 us -> 11.4 us  [the longest x1 9.02 us: local(): got = lax.ppermute(send, 'zh', swap)]
  transfers between devices with their start and end apart: 8 -> 10, of which waited for: 6 -> 5; matrix products, arithmetic and copies ran while one was open for 5% -> 5% of each run, Pallas kernels for 0% -> 8%
where the time goes in v2:
time: 113 us
  starting transfers between devices  43.9 us (39%)
  waiting for transfers between devices  28.3 us (25%)
  blocking collectives  18.5 us (16%)
  Pallas kernels  10.4 us (9%)
  local copies, waits for them, and re-layouts  5.62 us (5%)
  between operations  4.36 us (4%)
  other arithmetic  1.73 us (2%)
    all_to_all x1, blocking collectives, local(): kernel = lax.all_to_all(kernel, 'xz', 0, 0)  18.5 us
    pallas_call x4, Pallas kernels, call(): pl.pallas_call(kernel, out_shape=out_shape, in_specs=[SMEM] + [VMEM] * (l...  10.4 us
    ppermute x1, starting transfers between devices, local(): lax.ppermute(jnp.concatenate([grad.reshape(256, 128), wsend.reshape(432,...  9.73 us
    ppermute x1, waiting for transfers between devices, local(): got = lax.ppermute(send, 'zh', swap)  9.02 us
    all_to_all x1, waiting for transfers between devices, local(): lax.all_to_all(jnp.broadcast_to(slab[None], (8, 3, 8, 16, 128)), 'y', 0, 0)  8.5 us
    all_to_all x1, waiting for transfers between devices, local(): lax.all_to_all(jnp.broadcast_to(kernel[None], (16, 32, 128)), 'xz', 0, 0)  7.11 us
    all_to_all x1, starting transfers between devices, local(): lax.all_to_all(jnp.broadcast_to(slab[None], (8, 3, 8, 16, 128)), 'y', 0, 0)  6.83 us
    ppermute x1, starting transfers between devices, local(): rim = lax.ppermute(rim_of(fields[0], 0), ('xz', 'co'), near)[None]  5.52 us
  transfers between devices with their start and end apart: 10, of which 5 were waited for; matrix products, arithmetic and copies ran while one was open for 5% of the time, Pallas kernels for 8%

profile of v2, /device:TPU:1, one launch (start us, length us, event | category | flops | bytes accessed | tf_op | source)
XLA Modules:
  0.0 112.8 jit_solution(591181696164424654)
XLA Ops:
  0.6 0.9 copy_bitcast_fusion.1
  1.6 0.0 copy-start
  1.6 5.5 %collective-permute-start.1 = (bf16[8,16,128]{2,1,0:T(8,128)(2,1)S(1)}, bf16[8,16,128]{2,1,0:T(8,128)(2,1)S(1)}, u32[]{:S(2)}, u32[]{:S(2)}) collective-permute-start(bf16[8,16,128]{2,1,0:T(8,128)(2,1)S(1)} %dynamic-slice_bitcast_fusion), channel_id=1, source_target_pairs={{16,32},{48,64},{80,96},{112,128},{144,160},{176,192},{208,224},{2... | collective-permute-start | bytes 98312 | tf_op jit(solution)/shard_map/ppermute | solution.py:273
  7.2 0.1 pad_add_fusion.place
  7.3 0.0 copy-done
  7.3 0.8 shard_map.58
  8.1 9.7 %collective-permute-start = (bf16[688,128]{1,0:T(8,128)(2,1)S(1)}, bf16[688,128]{1,0:T(8,128)(2,1)S(1)}, u32[]{:S(2)}, u32[]{:S(2)}) collective-permute-start(bf16[688,128]{1,0:T(8,128)(2,1)S(1)} %pad_maximum_fusion.2), channel_id=1, source_target_pairs={{0,1},{1,0},{2,3},{3,2},{4,5},{5,4},{6,7},{7,6},{8,9},{9,8},{10,11... | collective-permute-start | bytes 528392 | tf_op jit(solution)/shard_map/ppermute | solution.py:254
  17.8 0.0 collective-permute-done.1
  17.8 1.1 broadcast_in_dim.6
  18.9 6.8 %all-to-all-start = ((bf16[8,3,8,16,128]{4,3,2,1,0:T(8,128)(2,1)}), bf16[8,3,8,16,128]{4,3,2,1,0:T(8,128)(2,1)S(1)}, u32[]{:S(2)}, u32[]{:S(2)}) async-start(bf16[8,3,8,16,128]{4,3,2,1,0:T(8,128)(2,1)} %broadcast_in_dim.6), calls=%async_computation | async-start | bytes 1572864 | tf_op jit(solution)/shard_map/all_to_all | solution.py:279
  25.7 0.0 collective-permute-done
  25.8 1.9 %collective-permute-start.2 = (bf16[2,2,8,16,128]{4,3,2,1,0:T(8,128)(2,1)S(1)}, bf16[2,2,8,16,128]{4,3,2,1,0:T(8,128)(2,1)S(1)}, u32[]{:S(2)}, u32[]{:S(2)}) collective-permute-start(bf16[2,2,8,16,128]{4,3,2,1,0:T(8,128)(2,1)S(1)} %pad_maximum_fusion.3), channel_id=1, source_target_pairs={{0,16},{16,0},{1,17},{17,1},{2,18},{18,2},{3,19},{19,3},{4,20},{20... | collective-permute-start | bytes 393224 | tf_op jit(solution)/shard_map/ppermute | solution.py:260
  27.7 3.5 %collective-permute-start.3 = (bf16[2,8,16,128]{3,2,1,0:T(8,128)(2,1)S(1)}, bf16[2,8,16,128]{3,2,1,0:T(8,128)(2,1)S(1)}, u32[]{:S(2)}, u32[]{:S(2)}) collective-permute-start(bf16[2,8,16,128]{3,2,1,0:T(8,128)(2,1)S(1)} %fusion.1), channel_id=1, source_target_pairs={{16,32},{48,64},{80,96},{112,128},{144,160},{176,192},{208,224},{2... | collective-permute-start | bytes 196616 | tf_op jit(solution)/shard_map/ppermute | solution.py:261
  31.2 2.4 %collective-permute-done.3.rim = bf16[2,8,16,128]{3,2,1,0:T(8,128)(2,1)S(1)} collective-permute-done((bf16[2,8,16,128]{3,2,1,0:T(8,128)(2,1)S(1)}, bf16[2,8,16,128]{3,2,1,0:T(8,128)(2,1)S(1)}, u32[]{:S(2)}, u32[]{:S(2)}) %collective-permute-start.3) | collective-permute-done | bytes 65568 | tf_op jit(solution)/shard_map/ppermute | solution.py:261
  33.6 0.0 collective-permute-done.2.other.cother
  33.6 3.6 %shard_map.59 = (f32[8,256,128]{2,1,0:T(8,128)S(1)}, f32[16,128]{1,0:T(8,128)S(1)}) custom-call(s32[3]{0:T(128)S(1)} %pad_add_fusion.place, bf16[27,16,128]{2,1,0:T(8,128)(2,1)S(1)} %get-tuple-element.15.wown, bf16[27,16,128]{2,1,0:T(8,128)(2,1)S(1)} %bitcast.49, bf16[2,8,16,128]{3,2,1,0:T(8,128)(2,1)S(1)} %get-tuple-element.40.own.cown, ...), custom_call_target="tpu_custom_call" | custom-call | flops 6000000000 | bytes 262144 | tf_op jit(solution)/shard_map/pallas_call | solution.py:21
  37.2 0.5 slice.57
  38.4 0.1 multiply_convert_fusion
  38.5 1.0 pad_maximum_fusion
  39.5 8.5 %all-to-all-done.vown = bf16[8,3,8,16,128]{4,3,2,1,0:T(8,128)(2,1)S(1)} async-done(((bf16[8,3,8,16,128]{4,3,2,1,0:T(8,128)(2,1)}), bf16[8,3,8,16,128]{4,3,2,1,0:T(8,128)(2,1)S(1)}, u32[]{:S(2)}, u32[]{:S(2)}) %all-to-all-start) | async-done | bytes 786464 | tf_op jit(solution)/shard_map/all_to_all | solution.py:279
  48.0 2.3 %collective-permute-start.4 = (bf16[8,3,8,16,128]{4,3,2,1,0:T(8,128)(2,1)S(1)}, bf16[8,3,8,16,128]{4,3,2,1,0:T(8,128)(2,1)S(1)}, u32[]{:S(2)}, u32[]{:S(2)}) collective-permute-start(bf16[8,3,8,16,128]{4,3,2,1,0:T(8,128)(2,1)S(1)} %all-to-all-done.vown), channel_id=1, source_target_pairs={{0,16},{16,0},{1,17},{17,1},{2,18},{18,2},{3,19},{19,3},{4,20},{20... | collective-permute-start | bytes 2359304 | tf_op jit(solution)/shard_map/ppermute | solution.py:281
  50.3 3.5 %all-to-all-start.1 = ((f16[8,272,128]{2,1,0:T(8,128)(2,1)}), f16[8,272,128]{2,1,0:T(8,128)(2,1)S(1)}, u32[]{:S(2)}, u32[]{:S(2)}) async-start(f16[8,272,128]{2,1,0:T(8,128)(2,1)} %pad_maximum_fusion), calls=%async_computation.1 | async-start | bytes 1114112 | tf_op jit(solution)/shard_map/all_to_all | solution.py:298
  53.9 0.0 collective-permute-done.4.vother
  53.9 4.4 %shard_map.60 = (f32[512,128]{1,0:T(8,128)S(1)}, f32[512,128]{1,0:T(8,128)S(1)}, f32[16,128]{1,0:T(8,128)S(1)}) custom-call(s32[3]{0:T(128)S(1)} %pad_add_fusion.place, bf16[27,16,128]{2,1,0:T(8,128)(2,1)S(1)} %get-tuple-element.15.wown, bf16[27,16,128]{2,1,0:T(8,128)(2,1)S(1)} %bitcast.50, bf16[8,3,8,16,128]{4,3,2,1,0:T(8,128)(2,1)S(1)} %all-to-all-done.vown, ...), custom_call_target="tpu_custom_call" | custom-call | flops 8000000000 | bytes 262144 | tf_op jit(solution)/shard_map/pallas_call | solution.py:21
  58.3 0.5 fusion.4
  60.3 1.9 %collective-permute-start.5 = (f16[528,128]{1,0:T(8,128)(2,1)S(1)}, f16[528,128]{1,0:T(8,128)(2,1)S(1)}, u32[]{:S(2)}, u32[]{:S(2)}) collective-permute-start(f16[528,128]{1,0:T(8,128)(2,1)S(1)} %pad_maximum_fusion.4), channel_id=1, source_target_pairs={{0,1},{1,0},{2,3},{3,2},{4,5},{5,4},{6,7},{7,6},{8,9},{9,8},{10,11... | collective-permute-start | bytes 405512 | tf_op jit(solution)/shard_map/ppermute | solution.py:297
  62.3 9.0 %collective-permute-done.5 = f16[528,128]{1,0:T(8,128)(2,1)S(1)} collective-permute-done((f16[528,128]{1,0:T(8,128)(2,1)S(1)}, f16[528,128]{1,0:T(8,128)(2,1)S(1)}, u32[]{:S(2)}, u32[]{:S(2)}) %collective-permute-start.5) | collective-permute-done | bytes 135200 | tf_op jit(solution)/shard_map/ppermute | solution.py:297
  71.3 1.2 %all-to-all-done.1 = f16[8,272,128]{2,1,0:T(8,128)(2,1)S(1)} async-done(((f16[8,272,128]{2,1,0:T(8,128)(2,1)}), f16[8,272,128]{2,1,0:T(8,128)(2,1)S(1)}, u32[]{:S(2)}, u32[]{:S(2)}) %all-to-all-start.1) | async-done | bytes 557088 | tf_op jit(solution)/shard_map/all_to_all | solution.py:298
  72.5 0.5 fusion.3
  74.5 18.5 %all_to_all.20 = f32[16,32,128]{2,1,0:T(8,128)S(1)} all-to-all(f32[16,32,128]{2,1,0:T(8,128)S(1)} %bitcast.53), channel_id=1, replica_groups=mesh['xz'=16,'co'=2,'y'=8,'zh'=2] {'xz'}, dimensions={0} | all-to-all | bytes 524288 | tf_op jit(solution)/shard_map/all_to_all | solution.py:302
  93.0 0.7 broadcast_in_dim.8
  93.7 4.0 %all-to-all-start.3 = ((bf16[16,32,128]{2,1,0:T(8,128)(2,1)}), bf16[16,32,128]{2,1,0:T(8,128)(2,1)S(1)}, u32[]{:S(2)}, u32[]{:S(2)}) async-start(bf16[16,32,128]{2,1,0:T(8,128)(2,1)} %broadcast_in_dim.8), calls=%async_computation.3 | async-start | bytes 262144 | tf_op jit(solution)/shard_map/all_to_all | solution.py:305
  97.7 0.2 exponential_reduce_fusion
  97.9 7.1 %all-to-all-done.3 = bf16[16,32,128]{2,1,0:T(8,128)(2,1)S(1)} async-done(((bf16[16,32,128]{2,1,0:T(8,128)(2,1)}), bf16[16,32,128]{2,1,0:T(8,128)(2,1)S(1)}, u32[]{:S(2)}, u32[]{:S(2)}) %all-to-all-start.3) | async-done | bytes 131104 | tf_op jit(solution)/shard_map/all_to_all | solution.py:305
  105.0 4.6 %collective-permute-start.6 = (bf16[2,16,16,128]{3,2,1,0:T(8,128)(2,1)S(1)}, bf16[2,16,16,128]{3,2,1,0:T(8,128)(2,1)S(1)}, u32[]{:S(2)}, u32[]{:S(2)}) collective-permute-start(bf16[2,16,16,128]{3,2,1,0:T(8,128)(2,1)S(1)} %bitcast.47), channel_id=1, source_target_pairs={{0,16},{16,0},{1,17},{17,1},{2,18},{18,2},{3,19},{19,3},{4,20},{20... | collective-permute-start | bytes 393224 | tf_op jit(solution)/shard_map/ppermute | solution.py:307
  109.6 0.2 multiply_reduce_fusion
  109.8 0.6 copy.16
  110.5 0.6 copy.20
  111.1 0.0 collective-permute-done.6.other
  111.1 1.7 %shard_map.61 = bf16[27,16,256]{2,1,0:T(8,128)(2,1)} custom-call(s32[3]{0:T(128)S(1)} %pad_add_fusion.place, bf16[2,16,16,128]{3,2,1,0:T(8,128)(2,1)S(1)} %bitcast.48, bf16[2,16,16,128]{3,2,1,0:T(8,128)(2,1)S(1)} %collective-permute-done.6.other), custom_call_target="tpu_custom_call" | custom-call | flops 1000000000 | bytes 262144 | tf_op jit(solution)/shard_map/pallas_call | solution.py:21
  (18 shorter events, 0.3 us)
Async XLA Ops:
  1.6 5.7 %copy-start = (bf16[16,3,3,3,256]{4,0,3,2,1:T(8,128)(2,1)S(1)}, bf16[16,3,3,3,256]{4,0,3,2,1:T(8,128)(2,1)}, u32[]{:S(2)}) copy-start(bf16[16,3,3,3,256]{4,0,3,2,1:T(8,128)(2,1)} %param.4) | copy-start | bytes 663556
  1.6 16.2 %collective-permute-start.1 = (bf16[8,16,128]{2,1,0:T(8,128)(2,1)S(1)}, bf16[8,16,128]{2,1,0:T(8,128)(2,1)S(1)}, u32[]{:S(2)}, u32[]{:S(2)}) collective-permute-start(bf16[8,16,128]{2,1,0:T(8,128)(2,1)S(1)} %dynamic-slice_bitcast_fusion), channel_id=1, source_target_pairs={{16,32},{48,64},{80,96},{112,128},{144,160},{176,192},{208,224},{2... | collective-permute-start | bytes 98312 | tf_op jit(solution)/shard_map/ppermute | solution.py:273
  8.1 17.7 %collective-permute-start = (bf16[688,128]{1,0:T(8,128)(2,1)S(1)}, bf16[688,128]{1,0:T(8,128)(2,1)S(1)}, u32[]{:S(2)}, u32[]{:S(2)}) collective-permute-start(bf16[688,128]{1,0:T(8,128)(2,1)S(1)} %pad_maximum_fusion.2), channel_id=1, source_target_pairs={{0,1},{1,0},{2,3},{3,2},{4,5},{5,4},{6,7},{7,6},{8,9},{9,8},{10,11... | collective-permute-start | bytes 528392 | tf_op jit(solution)/shard_map/ppermute | solution.py:254
  18.9 29.1 %all-to-all-start = ((bf16[8,3,8,16,128]{4,3,2,1,0:T(8,128)(2,1)}), bf16[8,3,8,16,128]{4,3,2,1,0:T(8,128)(2,1)S(1)}, u32[]{:S(2)}, u32[]{:S(2)}) async-start(bf16[8,3,8,16,128]{4,3,2,1,0:T(8,128)(2,1)} %broadcast_in_dim.6), calls=%async_computation | async-start | bytes 1572864 | tf_op jit(solution)/shard_map/all_to_all | solution.py:279
  25.8 7.8 %collective-permute-start.2 = (bf16[2,2,8,16,128]{4,3,2,1,0:T(8,128)(2,1)S(1)}, bf16[2,2,8,16,128]{4,3,2,1,0:T(8,128)(2,1)S(1)}, u32[]{:S(2)}, u32[]{:S(2)}) collective-permute-start(bf16[2,2,8,16,128]{4,3,2,1,0:T(8,128)(2,1)S(1)} %pad_maximum_fusion.3), channel_id=1, source_target_pairs={{0,16},{16,0},{1,17},{17,1},{2,18},{18,2},{3,19},{19,3},{4,20},{20... | collective-permute-start | bytes 393224 | tf_op jit(solution)/shard_map/ppermute | solution.py:260
  27.7 5.9 %collective-permute-start.3 = (bf16[2,8,16,128]{3,2,1,0:T(8,128)(2,1)S(1)}, bf16[2,8,16,128]{3,2,1,0:T(8,128)(2,1)S(1)}, u32[]{:S(2)}, u32[]{:S(2)}) collective-permute-start(bf16[2,8,16,128]{3,2,1,0:T(8,128)(2,1)S(1)} %fusion.1), channel_id=1, source_target_pairs={{16,32},{48,64},{80,96},{112,128},{144,160},{176,192},{208,224},{2... | collective-permute-start | bytes 196616 | tf_op jit(solution)/shard_map/ppermute | solution.py:261
  48.0 5.9 %collective-permute-start.4 = (bf16[8,3,8,16,128]{4,3,2,1,0:T(8,128)(2,1)S(1)}, bf16[8,3,8,16,128]{4,3,2,1,0:T(8,128)(2,1)S(1)}, u32[]{:S(2)}, u32[]{:S(2)}) collective-permute-start(bf16[8,3,8,16,128]{4,3,2,1,0:T(8,128)(2,1)S(1)} %all-to-all-done.vown), channel_id=1, source_target_pairs={{0,16},{16,0},{1,17},{17,1},{2,18},{18,2},{3,19},{19,3},{4,20},{20... | collective-permute-start | bytes 2359304 | tf_op jit(solution)/shard_map/ppermute | solution.py:281
  50.3 22.2 %all-to-all-start.1 = ((f16[8,272,128]{2,1,0:T(8,128)(2,1)}), f16[8,272,128]{2,1,0:T(8,128)(2,1)S(1)}, u32[]{:S(2)}, u32[]{:S(2)}) async-start(f16[8,272,128]{2,1,0:T(8,128)(2,1)} %pad_maximum_fusion), calls=%async_computation.1 | async-start | bytes 1114112 | tf_op jit(solution)/shard_map/all_to_all | solution.py:298
  60.3 11.0 %collective-permute-start.5 = (f16[528,128]{1,0:T(8,128)(2,1)S(1)}, f16[528,128]{1,0:T(8,128)(2,1)S(1)}, u32[]{:S(2)}, u32[]{:S(2)}) collective-permute-start(f16[528,128]{1,0:T(8,128)(2,1)S(1)} %pad_maximum_fusion.4), channel_id=1, source_target_pairs={{0,1},{1,0},{2,3},{3,2},{4,5},{5,4},{6,7},{7,6},{8,9},{9,8},{10,11... | collective-permute-start | bytes 405512 | tf_op jit(solution)/shard_map/ppermute | solution.py:297
  93.7 11.3 %all-to-all-start.3 = ((bf16[16,32,128]{2,1,0:T(8,128)(2,1)}), bf16[16,32,128]{2,1,0:T(8,128)(2,1)S(1)}, u32[]{:S(2)}, u32[]{:S(2)}) async-start(bf16[16,32,128]{2,1,0:T(8,128)(2,1)} %broadcast_in_dim.8), calls=%async_computation.3 | async-start | bytes 262144 | tf_op jit(solution)/shard_map/all_to_all | solution.py:305
  105.0 6.1 %collective-permute-start.6 = (bf16[2,16,16,128]{3,2,1,0:T(8,128)(2,1)S(1)}, bf16[2,16,16,128]{3,2,1,0:T(8,128)(2,1)S(1)}, u32[]{:S(2)}, u32[]{:S(2)}) collective-permute-start(bf16[2,16,16,128]{3,2,1,0:T(8,128)(2,1)S(1)} %bitcast.47), channel_id=1, source_target_pairs={{0,16},{16,0},{1,17},{17,1},{2,18},{18,2},{3,19},{19,3},{4,20},{20... | collective-permute-start | bytes 393224 | tf_op jit(solution)/shard_map/ppermute | solution.py:307

commit v3 on v2

--- a/solution.py
+++ b/solution.py
@@ -1,3 +1,4 @@
+import functools
 import math
 
 import jax
@@ -59,7 +60,7 @@
     dst[slot, row, 2] = jnp.where(lane == 127, 0.0, pltpu.roll(wide, 127, 1)).astype(BF)
 
 
-def data_kernel(place, wown, wgot, own, got, other, rim, out, power, planes, peak):
+def data_kernel(place, wown, wgot, own, got, other, rim, keep, send, planes, peak):
     j = place[0]
     zero = jnp.zeros((3, 32, 128), BF)
     for slot in range(4):
@@ -76,7 +77,8 @@
 
     lax.fori_loop(0, 8, fill, 0)
     peak[...] = jnp.zeros_like(peak)
-    same = jnp.where(iota((128, 128), 0) == iota((128, 128), 1), 1.0, 0.0).astype(BF)
+    turned = iota((128, 128), 0) ^ (16 * place[1])
+    pick = jnp.where(turned == iota((128, 128), 1), 1.0, 0.0).astype(BF)
     tiles = []
     for g in range(7):
         rows = []
@@ -84,7 +86,7 @@
             t = 26 - 4 * g - s
             rows += [wown[t], wgot[t]] if t >= 0 else [jnp.zeros((32, 128), BF)]
         tile = lax.dot_general(
-            same, jnp.concatenate(rows, axis=0), NT, preferred_element_type=F32
+            pick, jnp.concatenate(rows, axis=0), NT, preferred_element_type=F32
         )
         tiles.append(tile.astype(BF))
     lhs = jnp.concatenate(tiles, axis=1)
@@ -98,20 +100,32 @@
         rhs = jnp.concatenate([window(p, h), window(p, h + 1)], axis=1)
         res = jnp.dot(lhs, rhs, preferred_element_type=F32)
         at = (p * 8 + h) * 16
-        out[:, pl.ds(at, 16)] = res[:, :128].reshape(8, 16, 128)
-        out[:, pl.ds(at + 16, 16)] = res[:, 128:].reshape(8, 16, 128)
+        for m in range(8):
+            out = send if m % 2 else keep
+            rows = pl.ds(m // 2 * 256 + at, 16)
+            out[rows] = res[16 * m : 16 * m + 16, :128]
+            rows = pl.ds(m // 2 * 256 + at + 16, 16)
+            out[rows] = res[16 * m : 16 * m + 16, 128:]
         sizes = jnp.maximum(jnp.abs(res[:, :128]), jnp.abs(res[:, 128:]))
         peak[...] = jnp.maximum(peak[...], jnp.max(sizes.reshape(16, 8, 128), axis=0))
         return 0
 
     lax.fori_loop(0, 8, row_pair, 0)
     size = size_of(peak[...])
-    power[:8] = size
-    power[8:] = size
+    scale = jnp.exp2(14.0 - size)
+
+    def bring(step, _):
+        rows = pl.ds(pl.multiple_of(step * 64, 64), 64)
+        send[rows] = (send[rows].reshape(8, 8, 128) * scale).reshape(64, 128)
+        return 0
+
+    lax.fori_loop(0, 16, bring, 0)
+    send[1024:1032] = size
+    send[1032:1040] = size
 
 
 def volume_kernel(
-    place, wown, wgot, vown, vother, cown, cgot, cother, keep, send, power, planes, cot, resp, acc
+    place, wown, wgot, vown, vother, cown, cgot, cother, rkeep, rsend, taps, planes, cot, resp, acc
 ):
     j = place[0]
     cot[...] = jnp.zeros_like(cot)
@@ -145,14 +159,14 @@
     def row_pair(step, _):
         h = 2 * step
         for q in range(4):
-            taps = [a for a in range(3) if 0 <= q - a < 2]
-            lhs = weights[96 * taps[0] : 96 * taps[-1] + 96]
+            reach = [a for a in range(3) if 0 <= q - a < 2]
+            lhs = weights[96 * reach[0] : 96 * reach[-1] + 96]
             first = planes[2 * j + q, h].reshape(384, 128)
             second = planes[2 * j + q, h + 1].reshape(384, 128)
             res = jnp.dot(
                 lhs, jnp.concatenate([first, second], axis=1), preferred_element_type=F32
             )
-            for n, a in enumerate(taps):
+            for n, a in enumerate(reach):
                 for b in range(3):
                     at = 96 * n + 32 * b
                     resp[q - a, h + 2 - b] += res[at : at + 32, :128]
@@ -164,11 +178,18 @@
     for p in range(2):
         for h in range(8):
             at = (p * 8 + h) * 16
-            keep[at : at + 16] = resp[p, h + 1, :16]
+            rkeep[at : at + 16] = resp[p, h + 1, :16]
             part = resp[p, h + 1, 16:]
-            send[at : at + 16] = part
             peak = jnp.maximum(peak, jnp.max(jnp.abs(part).reshape(2, 8, 128), axis=0))
-    power[:8] = size_of(peak)
+    size = size_of(peak)
+    scale = jnp.exp2(14.0 - size)
+    for p in range(2):
+        for h in range(8):
+            at = (p * 8 + h) * 16
+            part = resp[p, h + 1, 16:].reshape(2, 8, 128) * scale
+            rsend[at : at + 16] = part.reshape(16, 128)
+    rsend[256:264] = size
+    rsend[264:272] = size
 
     acc[...] = jnp.zeros_like(acc)
     for q in range(6):
@@ -177,8 +198,8 @@
         for h in range(8):
             grads = cot[q + low : q + high + 1, h : h + 3]
             lhs.append(grads.reshape(96 * (high - low + 1), 128))
-            taps = planes[q, h, :, half].reshape(192, 128)
-            rhs.append(jnp.concatenate([taps, jnp.zeros((64, 128), BF)], axis=0))
+            shifted = planes[q, h, :, half].reshape(192, 128)
+            rhs.append(jnp.concatenate([shifted, jnp.zeros((64, 128), BF)], axis=0))
         res = lax.dot_general(
             jnp.concatenate(lhs, axis=1),
             jnp.concatenate(rhs, axis=1),
@@ -186,33 +207,39 @@
             preferred_element_type=F32,
         )
         acc[96 * low : 96 * high + 96] += res
-    for side, out in enumerate((keep, send)):
-        third = []
+    for side in range(2):
+        tiles, third = [], []
         for ab in range(9):
             rows = pl.ds(32 * ab + 16 * side, 16)
-            out[256 + 16 * ab : 272 + 16 * ab] = acc[rows, :128]
+            tiles.append(acc[rows, :128])
             third.append(acc[rows, 128:])
-        for n in range(5):
-            tile = third[2 * n]
-            if n < 4:
-                tile = tile + pltpu.roll(third[2 * n + 1], 64, 1)
-            out[400 + 16 * n : 416 + 16 * n] = tile
-        out[480:512] = jnp.zeros((32, 128), F32)
-    peak = jnp.max(jnp.abs(send[256:480]).reshape(28, 8, 128), axis=0)
-    power[8:] = size_of(peak)
+        for n in range(4):
+            tiles.append(third[2 * n] + pltpu.roll(third[2 * n + 1], 64, 1))
+        tiles.append(third[8])
+        for r, tile in enumerate(tiles):
+            at = 32 * r + 16 * side
+            taps[at : at + 16] = tile
+    taps[448:512] = jnp.zeros((64, 128), F32)
+
+
+def sum_kernel(factor, place, parts, out):
+    total = parts[0]
+    for n in range(1, 16):
+        total = total + parts[n]
+    out[...] = (total * factor).astype(BF)
 
 
 def place_kernel(place, own, other, out):
-    j, zh = place[0], place[2]
+    j = place[0]
     lane, n = iota((128, 512), 0), iota((128, 512), 1)
     y, z, i, s = n % 256 // 32, n % 32 // 16, n % 16, n // 256
     source = s * 64 + y % 4 * 16 + i
     total = jnp.zeros((224, 512), F32)
     for core, ref in enumerate((own, other)):
-        for turn in range(2):
-            hit = (lane == source) & (y // 4 == (j ^ core)) & ((z ^ zh) == turn)
+        for side in range(2):
+            hit = (lane == source) & (y // 4 == (j ^ core)) & (z == side)
             pick = jnp.where(hit, 1.0, 0.0).astype(BF)
-            part = ref[turn, :14].reshape(224, 128)
+            part = ref[:14, side].reshape(224, 128)
             total = total + jnp.dot(part, pick, preferred_element_type=F32)
     for r in range(14):
         for s in range(2):
@@ -223,12 +250,26 @@
             out[t] = total[16 * r : 16 * r + 16, 256 * s : 256 * s + 256].astype(BF)
 
 
-def shrink(value, power):
-    return (value * jnp.exp2(14.0 - power)).astype(F16)
-
-
 def grow(value, power):
     return value.astype(F32) * jnp.exp2(power.astype(F32) - 14.0)
+
+
+def split(total, power):
+    count = total.shape[0] // 2
+    send = (total[1::2] * jnp.exp2(14.0 - power)).reshape(count * 256, 128)
+    return total[::2], jnp.concatenate([send, jnp.broadcast_to(power, (16, 128))])
+
+
+def exchange(total, send, turn):
+    got = lax.ppermute(send.astype(F16), "y", [(i, i ^ turn) for i in range(8)])
+    return merge(total, send, got)
+
+
+def merge(total, send, got):
+    count = total.shape[0]
+    theirs = got[256 * count : 256 * count + 1]
+    total = total + grow(got[: 256 * count], theirs).reshape(count, 256, 128)
+    return total, jnp.maximum(send[256 * count : 256 * count + 1], theirs.astype(F32)) + 1.0
 
 
 def local(volume, filters, cotangent):
@@ -260,15 +301,12 @@
     grad_other = lax.ppermute(both, "co", swap)
     grad_rim = lax.ppermute(rim_of(both, 1), ("xz", "co"), near)
 
-    data, size = call(
+    data_keep, data_send = call(
         data_kernel,
-        [jax.ShapeDtypeStruct((8, 256, 128), F32), jax.ShapeDtypeStruct((16, 128), F32)],
+        [jax.ShapeDtypeStruct((1024, 128), F32), jax.ShapeDtypeStruct((1040, 128), F32)],
         [place, wown, wgot, grad, grad_got, grad_other, grad_rim],
         [pltpu.VMEM((4, 10, 3, 32, 128), BF), pltpu.VMEM((8, 128), F32)],
-        micros=6,
-    )
-    data = jnp.concatenate(
-        [shrink(data, size[0, 0]), jnp.broadcast_to(size[None].astype(F16), (8, 16, 128))], axis=1
+        micros=10,
     )
     rim = lax.ppermute(rim_of(fields[0], 0), ("xz", "co"), near)[None]
     slab = jnp.where(
@@ -277,11 +315,12 @@
         jnp.concatenate([fields[0], rim], axis=0),
     )
     vol = lax.all_to_all(jnp.broadcast_to(slab[None], (8, 3, 8, 16, 128)), "y", 0, 0)
-    vol, data = lax.optimization_barrier((vol, data))
+    vol, data_keep, data_send = lax.optimization_barrier((vol, data_keep, data_send))
     vol_other = lax.ppermute(vol, "co", swap)
-    keep, send, size = call(
+    data_got = lax.ppermute(data_send.astype(F16), "y", [(i, i ^ 1) for i in range(8)])
+    rkeep, rsend, taps = call(
         volume_kernel,
-        [jax.ShapeDtypeStruct((512, 128), F32)] * 2 + [jax.ShapeDtypeStruct((16, 128), F32)],
+        [jax.ShapeDtypeStruct((rows, 128), F32) for rows in (256, 272, 512)],
         [place, wown, wgot, vol, vol_other, grad, grad_got, grad_other],
         [
             pltpu.VMEM((6, 8, 3, 128, 128), BF),
@@ -291,26 +330,34 @@
         ],
         micros=8,
     )
-    send = jnp.concatenate(
-        [shrink(send[:256], size[0, 0]), shrink(send[256:], size[8, 0]), size.astype(F16)]
-    )
-    got = lax.ppermute(send, "zh", swap)
-    data = lax.all_to_all(data, "y", 0, 0)
-    keep, got, data = lax.optimization_barrier((keep, got, data))
-
-    kernel = jnp.concatenate([keep[256:], grow(got[256:512], got[520, 0])]).reshape(16, 32, 128)
-    kernel = lax.all_to_all(kernel, "xz", 0, 0)
-    factor = 1.0 / math.sqrt(cells)
-    kernel = (jnp.sum(kernel, axis=0) * factor).astype(BF)
-    kernel = lax.all_to_all(jnp.broadcast_to(kernel[None], (16, 32, 128)), "xz", 0, 0)
-    kernel = kernel.reshape(2, 16, 16, 128)
+    kernel = lax.all_to_all(taps.reshape(16, 32, 128), "xz", 0, 0)
+    got = lax.ppermute(rsend.astype(F16), "zh", swap)
+
+    kernel, data_got1 = lax.optimization_barrier((kernel, data_got))
+    kernel = call(
+        functools.partial(sum_kernel, 1.0 / math.sqrt(cells)),
+        jax.ShapeDtypeStruct((32, 128), BF),
+        [place, kernel],
+    )
+    data, power = merge(data_keep.reshape(4, 256, 128), data_send, data_got1)
+    data, power = exchange(*split(data, power), 2)
+    data_keep, data_send = split(data, power)
+    data_got = lax.ppermute(data_send.astype(F16), "y", [(i, i ^ 4) for i in range(8)])
+
+    halves = kernel.reshape(2, 16, 128)
+    halves = jnp.where(lax.axis_index("zh") == 0, halves, halves[::-1])
+    kernel = jnp.broadcast_to(halves[None], (16, 2, 16, 128)).reshape(32, 16, 128)
+    kernel = lax.all_to_all(kernel, ("xz", "zh"), 0, 0).reshape(16, 2, 16, 128)
+    kernel, got = lax.optimization_barrier((kernel, got))
+    response = (rkeep + grow(got[:256], got[256:257])).reshape(2, 8, 16, 128)
     kernel_other = lax.ppermute(kernel, "co", swap)
+    kernel_other, data_got = lax.optimization_barrier((kernel_other, data_got))
+    data, power = merge(data_keep, data_send, data_got)
+    data = data.reshape(2, 8, 16, 128)
     placed = call(
         place_kernel, jax.ShapeDtypeStruct((27, 16, 256), BF), [place, kernel, kernel_other]
     )
     order = (2, 0, 1, 3)
-    response = (keep[:256] + grow(got[:256], got[512, 0])).reshape(2, 8, 16, 128)
-    data = jnp.sum(grow(data[:, :256], data[:, 256:257, :1]), axis=0).reshape(2, 8, 16, 128)
     return (
         jnp.transpose(response.astype(BF), order),
         jnp.transpose(data.astype(BF), order),

time: 113 us -> 104 us (0.920)
  blocking collectives: 18.5 us -> 0 us
  starting transfers between devices: 43.9 us -> 59.3 us
  between operations: 4.36 us -> 0.98 us
  waiting for transfers between devices: 28.3 us -> 26.7 us
  local copies, waits for them, and re-layouts: 5.62 us -> 4.02 us
  Pallas kernels: 10.4 us -> 11.7 us
  other arithmetic: 1.73 us -> 0.56 us
    all_to_all x1 -> x0, blocking collectives: 18.5 us -> none  [local(): kernel = lax.all_to_all(kernel, 'xz', 0, 0)]
    ppermute x1 -> x4, starting transfers between devices: 1.92 us -> 9.6 us  [the longest x1 3.42 us: local(): lax.ppermute(data_send.astype(F16), 'y', [(i, i ^ 4) for i in range(8)])]
    all_to_all x2, starting transfers between devices: 7.56 us -> 14.3 us  [the longest x1 8.03 us: local(): kernel = lax.all_to_all(taps.reshape(16, 32, 128), 'xz', 0, 0)]
    ppermute x1 -> x4, waiting for transfers between devices: 9.02 us -> 5.55 us  [the longest x1 4.96 us: local(): lax.ppermute(data_send.astype(F16), 'y', [(i, i ^ 1) for i in range(8)])]
    all_to_all x2, waiting for transfers between devices: 8.36 us -> 5.88 us  [the longest x1 5.19 us: local(): kernel = lax.all_to_all(kernel, ('xz', 'zh'), 0, 0).reshape(16, 2, 16, 128)]
    all_to_all x1, waiting for transfers between devices: 8.5 us -> 10.7 us  [local(): lax.all_to_all(jnp.broadcast_to(slab[None], (8, 3, 8, 16, 128)), 'y', 0, 0)]
    ppermute x1, waiting for transfers between devices: 0.01 us -> 1.89 us  [local(): vol_other = lax.ppermute(vol, 'co', swap)]
    slice x3 -> x0, local copies, waits for them, and re-layouts: 1.58 us -> none  [the longest x2 1.06 us: local(): size[0, 0]]
  transfers between devices with their start and end apart: 10 -> 13, of which waited for: 5 -> 8; matrix products, arithmetic and copies ran while one was open for 5% -> 3% of each run, Pallas kernels for 8% -> 5%
where the time goes in v3:
time: 104 us; the launch traced here: 103 us
  starting transfers between devices  59.3 us (57%)
  waiting for transfers between devices  26.7 us (26%)
  Pallas kernels  11.7 us (11%)
  local copies, waits for them, and re-layouts  4.02 us (4%)
    pallas_call x5, Pallas kernels, call(): pl.pallas_call(kernel, out_shape=out_shape, in_specs=[SMEM] + [VMEM] * (l...  11.7 us
    all_to_all x1, waiting for transfers between devices, local(): lax.all_to_all(jnp.broadcast_to(slab[None], (8, 3, 8, 16, 128)), 'y', 0, 0)  10.7 us
    ppermute x1, starting transfers between devices, local(): lax.ppermute(jnp.concatenate([grad.reshape(256, 128), wsend.reshape(432,...  9.73 us
    all_to_all x1, starting transfers between devices, local(): kernel = lax.all_to_all(taps.reshape(16, 32, 128), 'xz', 0, 0)  8.03 us
    all_to_all x1, starting transfers between devices, local(): lax.all_to_all(jnp.broadcast_to(slab[None], (8, 3, 8, 16, 128)), 'y', 0, 0)  6.83 us
    all_to_all x1, starting transfers between devices, local(): kernel = lax.all_to_all(kernel, ('xz', 'zh'), 0, 0).reshape(16, 2, 16, 128)  6.23 us
    ppermute x1, starting transfers between devices, local(): kernel_other = lax.ppermute(kernel, 'co', swap)  5.63 us
    ppermute x1, starting transfers between devices, local(): rim = lax.ppermute(rim_of(fields[0], 0), ('xz', 'co'), near)[None]  5.52 us
  transfers between devices with their start and end apart: 13, of which 8 were waited for; matrix products, arithmetic and copies ran while one was open for 3% of the time, Pallas kernels for 5%

profile of v3, /device:TPU:1, one launch (start us, length us, event | category | flops | bytes accessed | tf_op | source)
XLA Modules:
  0.0 103.2 jit_solution(10313758668099336766)
XLA Ops:
  0.6 0.9 copy_bitcast_fusion.2
  1.6 0.0 copy-start
  1.6 5.5 %collective-permute-start.1 = (bf16[8,16,128]{2,1,0:T(8,128)(2,1)S(1)}, bf16[8,16,128]{2,1,0:T(8,128)(2,1)S(1)}, u32[]{:S(2)}, u32[]{:S(2)}) collective-permute-start(bf16[8,16,128]{2,1,0:T(8,128)(2,1)S(1)} %dynamic-slice_bitcast_fusion), channel_id=1, source_target_pairs={{16,32},{48,64},{80,96},{112,128},{144,160},{176,192},{208,224},{2... | collective-permute-start | bytes 98312 | tf_op jit(solution)/shard_map/ppermute | solution.py:311
  7.2 0.1 pad_add_fusion.place
  7.3 0.0 copy-done
  7.3 0.8 shard_map.58
  8.1 9.7 %collective-permute-start = (bf16[688,128]{1,0:T(8,128)(2,1)S(1)}, bf16[688,128]{1,0:T(8,128)(2,1)S(1)}, u32[]{:S(2)}, u32[]{:S(2)}) collective-permute-start(bf16[688,128]{1,0:T(8,128)(2,1)S(1)} %pad_maximum_fusion), channel_id=1, source_target_pairs={{0,1},{1,0},{2,3},{3,2},{4,5},{5,4},{6,7},{7,6},{8,9},{9,8},{10,11... | collective-permute-start | bytes 528392 | tf_op jit(solution)/shard_map/ppermute | solution.py:295
  17.8 0.0 collective-permute-done.1
  17.8 1.1 %broadcast_in_dim.12 = bf16[8,3,8,16,128]{4,3,2,1,0:T(8,128)(2,1)} broadcast(bf16[3,8,16,128]{3,2,1,0:T(8,128)(2,1)S(1)} %maximum_select_fusion), dimensions={1,2,3,4} | broadcast | bytes 884736 | tf_op jit(solution)/shard_map/broadcast_in_dim | solution.py:317
  18.9 6.8 %all-to-all-start = ((bf16[8,3,8,16,128]{4,3,2,1,0:T(8,128)(2,1)}), bf16[8,3,8,16,128]{4,3,2,1,0:T(8,128)(2,1)S(1)}, u32[]{:S(2)}, u32[]{:S(2)}) async-start(bf16[8,3,8,16,128]{4,3,2,1,0:T(8,128)(2,1)} %broadcast_in_dim.12), calls=%async_computation | async-start | bytes 1572864 | tf_op jit(solution)/shard_map/all_to_all | solution.py:317
  25.7 0.0 collective-permute-done
  25.8 1.9 %collective-permute-start.2 = (bf16[2,2,8,16,128]{4,3,2,1,0:T(8,128)(2,1)S(1)}, bf16[2,2,8,16,128]{4,3,2,1,0:T(8,128)(2,1)S(1)}, u32[]{:S(2)}, u32[]{:S(2)}) collective-permute-start(bf16[2,2,8,16,128]{4,3,2,1,0:T(8,128)(2,1)S(1)} %pad_maximum_fusion.1), channel_id=1, source_target_pairs={{0,16},{16,0},{1,17},{17,1},{2,18},{18,2},{3,19},{19,3},{4,20},{20... | collective-permute-start | bytes 393224 | tf_op jit(solution)/shard_map/ppermute | solution.py:301
  27.7 3.5 %collective-permute-start.3 = (bf16[2,8,16,128]{3,2,1,0:T(8,128)(2,1)S(1)}, bf16[2,8,16,128]{3,2,1,0:T(8,128)(2,1)S(1)}, u32[]{:S(2)}, u32[]{:S(2)}) collective-permute-start(bf16[2,8,16,128]{3,2,1,0:T(8,128)(2,1)S(1)} %fusion.4), channel_id=1, source_target_pairs={{16,32},{48,64},{80,96},{112,128},{144,160},{176,192},{208,224},{2... | collective-permute-start | bytes 196616 | tf_op jit(solution)/shard_map/ppermute | solution.py:302
  31.2 2.4 %collective-permute-done.3.rim = bf16[2,8,16,128]{3,2,1,0:T(8,128)(2,1)S(1)} collective-permute-done((bf16[2,8,16,128]{3,2,1,0:T(8,128)(2,1)S(1)}, bf16[2,8,16,128]{3,2,1,0:T(8,128)(2,1)S(1)}, u32[]{:S(2)}, u32[]{:S(2)}) %collective-permute-start.3) | collective-permute-done | bytes 65568 | tf_op jit(solution)/shard_map/ppermute | solution.py:302
  33.6 0.0 collective-permute-done.2.other.cother
  33.6 3.7 %shard_map.59 = (f32[1024,128]{1,0:T(8,128)S(1)}, f32[1040,128]{1,0:T(8,128)S(1)}) custom-call(s32[3]{0:T(128)S(1)} %pad_add_fusion.place, bf16[27,16,128]{2,1,0:T(8,128)(2,1)S(1)} %get-tuple-element.19.wown, bf16[27,16,128]{2,1,0:T(8,128)(2,1)S(1)} %bitcast.70, bf16[2,8,16,128]{3,2,1,0:T(8,128)(2,1)S(1)} %get-tuple-element.41.own.cown, ...), custom_call_target="tpu_custom_call" | custom-call | flops 10000000000 | bytes 262144 | tf_op jit(solution)/shard_map/pallas_call | solution.py:22
  37.3 10.7 %all-to-all-done.vown = bf16[8,3,8,16,128]{4,3,2,1,0:T(8,128)(2,1)S(1)} async-done(((bf16[8,3,8,16,128]{4,3,2,1,0:T(8,128)(2,1)}), bf16[8,3,8,16,128]{4,3,2,1,0:T(8,128)(2,1)S(1)}, u32[]{:S(2)}, u32[]{:S(2)}) %all-to-all-start) | async-done | bytes 786464 | tf_op jit(solution)/shard_map/all_to_all | solution.py:317
  48.0 2.3 %collective-permute-start.4 = (bf16[8,3,8,16,128]{4,3,2,1,0:T(8,128)(2,1)S(1)}, bf16[8,3,8,16,128]{4,3,2,1,0:T(8,128)(2,1)S(1)}, u32[]{:S(2)}, u32[]{:S(2)}) collective-permute-start(bf16[8,3,8,16,128]{4,3,2,1,0:T(8,128)(2,1)S(1)} %all-to-all-done.vown), channel_id=1, source_target_pairs={{0,16},{16,0},{1,17},{17,1},{2,18},{18,2},{3,19},{19,3},{4,20},{20... | collective-permute-start | bytes 2359304 | tf_op jit(solution)/shard_map/ppermute | solution.py:319
  50.3 1.9 %collective-permute-done.4.vother = bf16[8,3,8,16,128]{4,3,2,1,0:T(8,128)(2,1)S(1)} collective-permute-done((bf16[8,3,8,16,128]{4,3,2,1,0:T(8,128)(2,1)S(1)}, bf16[8,3,8,16,128]{4,3,2,1,0:T(8,128)(2,1)S(1)}, u32[]{:S(2)}, u32[]{:S(2)}) %collective-permute-start.4) | collective-permute-done | bytes 786464 | tf_op jit(solution)/shard_map/ppermute | solution.py:319
  52.2 5.0 %shard_map.60 = (f32[256,128]{1,0:T(8,128)S(1)}, f32[272,128]{1,0:T(8,128)S(1)}, f32[512,128]{1,0:T(8,128)}) custom-call(s32[3]{0:T(128)S(1)} %pad_add_fusion.place, bf16[27,16,128]{2,1,0:T(8,128)(2,1)S(1)} %get-tuple-element.19.wown, bf16[27,16,128]{2,1,0:T(8,128)(2,1)S(1)} %bitcast.71, bf16[8,3,8,16,128]{4,3,2,1,0:T(8,128)(2,1)S(1)} %all-to-all-done.vown, ...), custom_call_target="tpu_custom_call" | custom-call | flops 8000000000 | bytes 262144 | tf_op jit(solution)/shard_map/pallas_call | solution.py:22
  57.2 8.0 %all-to-all-start.1 = ((f32[16,32,128]{2,1,0:T(8,128)}), f32[16,32,128]{2,1,0:T(8,128)S(1)}, u32[]{:S(2)}, u32[]{:S(2)}) async-start(f32[16,32,128]{2,1,0:T(8,128)} %bitcast.18), calls=%async_computation.1 | async-start | bytes 524288 | tf_op jit(solution)/shard_map/all_to_all | solution.py:333
  65.3 2.1 %collective-permute-start.5 = (f16[1040,128]{1,0:T(8,128)(2,1)S(1)}, f16[1040,128]{1,0:T(8,128)(2,1)S(1)}, u32[]{:S(2)}, u32[]{:S(2)}) collective-permute-start(f16[1040,128]{1,0:T(8,128)(2,1)S(1)} %convert_element_type.46), channel_id=1, source_target_pairs={{0,2},{2,0},{4,6},{6,4},{8,10},{10,8},{12,14},{14,12},{1,3},{3,1},... | collective-permute-start | bytes 798728 | tf_op jit(solution)/shard_map/ppermute | solution.py:320
  67.5 2.1 %collective-permute-start.6 = (f16[272,128]{1,0:T(8,128)(2,1)S(1)}, f16[272,128]{1,0:T(8,128)(2,1)S(1)}, u32[]{:S(2)}, u32[]{:S(2)}) collective-permute-start(f16[272,128]{1,0:T(8,128)(2,1)S(1)} %convert_element_type.47), channel_id=1, source_target_pairs={{0,1},{1,0},{2,3},{3,2},{4,5},{5,4},{6,7},{7,6},{8,9},{9,8},{10,11... | collective-permute-start | bytes 208904 | tf_op jit(solution)/shard_map/ppermute | solution.py:334
  69.5 5.0 %collective-permute-done.5 = f16[1040,128]{1,0:T(8,128)(2,1)S(1)} collective-permute-done((f16[1040,128]{1,0:T(8,128)(2,1)S(1)}, f16[1040,128]{1,0:T(8,128)(2,1)S(1)}, u32[]{:S(2)}, u32[]{:S(2)}) %collective-permute-start.5) | collective-permute-done | bytes 266272 | tf_op jit(solution)/shard_map/ppermute | solution.py:320
  74.5 0.7 all-to-all-done.1.parts
  75.2 0.1 multiply_add_fusion
  75.4 2.0 %collective-permute-start.7 = (f16[528,128]{1,0:T(8,128)(2,1)S(1)}, f16[528,128]{1,0:T(8,128)(2,1)S(1)}, u32[]{:S(2)}, u32[]{:S(2)}) collective-permute-start(f16[528,128]{1,0:T(8,128)(2,1)S(1)} %pad_maximum_fusion.2), channel_id=1, source_target_pairs={{0,4},{2,6},{4,0},{6,2},{8,12},{10,14},{12,8},{14,10},{1,5},{3,7},... | collective-permute-start | bytes 405512 | tf_op jit(solution)/shard_map/ppermute | solution.py:264
  77.4 0.6 shard_map.61
  78.0 0.7 broadcast_in_dim.13
  78.7 6.2 %all-to-all-start.2 = ((bf16[32,16,128]{2,1,0:T(8,128)(2,1)}), bf16[32,16,128]{2,1,0:T(8,128)(2,1)S(1)}, u32[]{:S(2)}, u32[]{:S(2)}) async-start(bf16[32,16,128]{2,1,0:T(8,128)(2,1)} %bitcast.20), calls=%async_computation.2 | async-start | bytes 262144 | tf_op jit(solution)/shard_map/all_to_all | solution.py:350
  84.9 0.6 collective-permute-done.7
  85.6 3.4 %collective-permute-start.9 = (f16[272,128]{1,0:T(8,128)(2,1)S(1)}, f16[272,128]{1,0:T(8,128)(2,1)S(1)}, u32[]{:S(2)}, u32[]{:S(2)}) collective-permute-start(f16[272,128]{1,0:T(8,128)(2,1)S(1)} %pad_maximum_fusion.3), channel_id=1, source_target_pairs={{0,8},{2,10},{4,12},{6,14},{8,0},{10,2},{12,4},{14,6},{1,9},{3,11}... | collective-permute-start | bytes 208904 | tf_op jit(solution)/shard_map/ppermute | solution.py:345
  89.0 0.0 collective-permute-done.6
  89.1 5.2 %all-to-all-done.2 = bf16[32,16,128]{2,1,0:T(8,128)(2,1)S(1)} async-done(((bf16[32,16,128]{2,1,0:T(8,128)(2,1)}), bf16[32,16,128]{2,1,0:T(8,128)(2,1)S(1)}, u32[]{:S(2)}, u32[]{:S(2)}) %all-to-all-start.2) | async-done | bytes 131104 | tf_op jit(solution)/shard_map/all_to_all | solution.py:350
  94.3 5.6 %collective-permute-start.8 = (bf16[16,2,16,128]{3,2,1,0:T(8,128)(2,1)S(1)}, bf16[16,2,16,128]{3,2,1,0:T(8,128)(2,1)S(1)}, u32[]{:S(2)}, u32[]{:S(2)}) collective-permute-start(bf16[16,2,16,128]{3,2,1,0:T(8,128)(2,1)S(1)} %bitcast.68), channel_id=1, source_target_pairs={{0,16},{16,0},{1,17},{17,1},{2,18},{18,2},{3,19},{19,3},{4,20},{20... | collective-permute-start | bytes 393224 | tf_op jit(solution)/shard_map/ppermute | solution.py:353
  99.9 0.6 copy.15
  100.6 0.0 collective-permute-done.9
  100.6 0.3 collective-permute-done.8.other
  100.9 1.7 %shard_map.62 = bf16[27,16,256]{2,1,0:T(8,128)(2,1)} custom-call(s32[3]{0:T(128)S(1)} %pad_add_fusion.place, bf16[16,2,16,128]{3,2,1,0:T(8,128)(2,1)S(1)} %bitcast.69, bf16[16,2,16,128]{3,2,1,0:T(8,128)(2,1)S(1)} %collective-permute-done.8.other), custom_call_target="tpu_custom_call" | custom-call | flops 1000000000 | bytes 262144 | tf_op jit(solution)/shard_map/pallas_call | solution.py:22
  102.6 0.6 copy.14
  (27 shorter events, 0.5 us)
Async XLA Ops:
  1.6 5.7 %copy-start = (bf16[16,3,3,3,256]{4,0,3,2,1:T(8,128)(2,1)S(1)}, bf16[16,3,3,3,256]{4,0,3,2,1:T(8,128)(2,1)}, u32[]{:S(2)}) copy-start(bf16[16,3,3,3,256]{4,0,3,2,1:T(8,128)(2,1)} %param.4) | copy-start | bytes 663556
  1.6 16.2 %collective-permute-start.1 = (bf16[8,16,128]{2,1,0:T(8,128)(2,1)S(1)}, bf16[8,16,128]{2,1,0:T(8,128)(2,1)S(1)}, u32[]{:S(2)}, u32[]{:S(2)}) collective-permute-start(bf16[8,16,128]{2,1,0:T(8,128)(2,1)S(1)} %dynamic-slice_bitcast_fusion), channel_id=1, source_target_pairs={{16,32},{48,64},{80,96},{112,128},{144,160},{176,192},{208,224},{2... | collective-permute-start | bytes 98312 | tf_op jit(solution)/shard_map/ppermute | solution.py:311
  8.1 17.7 %collective-permute-start = (bf16[688,128]{1,0:T(8,128)(2,1)S(1)}, bf16[688,128]{1,0:T(8,128)(2,1)S(1)}, u32[]{:S(2)}, u32[]{:S(2)}) collective-permute-start(bf16[688,128]{1,0:T(8,128)(2,1)S(1)} %pad_maximum_fusion), channel_id=1, source_target_pairs={{0,1},{1,0},{2,3},{3,2},{4,5},{5,4},{6,7},{7,6},{8,9},{9,8},{10,11... | collective-permute-start | bytes 528392 | tf_op jit(solution)/shard_map/ppermute | solution.py:295
  18.9 29.1 %all-to-all-start = ((bf16[8,3,8,16,128]{4,3,2,1,0:T(8,128)(2,1)}), bf16[8,3,8,16,128]{4,3,2,1,0:T(8,128)(2,1)S(1)}, u32[]{:S(2)}, u32[]{:S(2)}) async-start(bf16[8,3,8,16,128]{4,3,2,1,0:T(8,128)(2,1)} %broadcast_in_dim.12), calls=%async_computation | async-start | bytes 1572864 | tf_op jit(solution)/shard_map/all_to_all | solution.py:317
  25.8 7.8 %collective-permute-start.2 = (bf16[2,2,8,16,128]{4,3,2,1,0:T(8,128)(2,1)S(1)}, bf16[2,2,8,16,128]{4,3,2,1,0:T(8,128)(2,1)S(1)}, u32[]{:S(2)}, u32[]{:S(2)}) collective-permute-start(bf16[2,2,8,16,128]{4,3,2,1,0:T(8,128)(2,1)S(1)} %pad_maximum_fusion.1), channel_id=1, source_target_pairs={{0,16},{16,0},{1,17},{17,1},{2,18},{18,2},{3,19},{19,3},{4,20},{20... | collective-permute-start | bytes 393224 | tf_op jit(solution)/shard_map/ppermute | solution.py:301
  27.7 5.9 %collective-permute-start.3 = (bf16[2,8,16,128]{3,2,1,0:T(8,128)(2,1)S(1)}, bf16[2,8,16,128]{3,2,1,0:T(8,128)(2,1)S(1)}, u32[]{:S(2)}, u32[]{:S(2)}) collective-permute-start(bf16[2,8,16,128]{3,2,1,0:T(8,128)(2,1)S(1)} %fusion.4), channel_id=1, source_target_pairs={{16,32},{48,64},{80,96},{112,128},{144,160},{176,192},{208,224},{2... | collective-permute-start | bytes 196616 | tf_op jit(solution)/shard_map/ppermute | solution.py:302
  48.0 4.2 %collective-permute-start.4 = (bf16[8,3,8,16,128]{4,3,2,1,0:T(8,128)(2,1)S(1)}, bf16[8,3,8,16,128]{4,3,2,1,0:T(8,128)(2,1)S(1)}, u32[]{:S(2)}, u32[]{:S(2)}) collective-permute-start(bf16[8,3,8,16,128]{4,3,2,1,0:T(8,128)(2,1)S(1)} %all-to-all-done.vown), channel_id=1, source_target_pairs={{0,16},{16,0},{1,17},{17,1},{2,18},{18,2},{3,19},{19,3},{4,20},{20... | collective-permute-start | bytes 2359304 | tf_op jit(solution)/shard_map/ppermute | solution.py:319
  57.2 17.9 %all-to-all-start.1 = ((f32[16,32,128]{2,1,0:T(8,128)}), f32[16,32,128]{2,1,0:T(8,128)S(1)}, u32[]{:S(2)}, u32[]{:S(2)}) async-start(f32[16,32,128]{2,1,0:T(8,128)} %bitcast.18), calls=%async_computation.1 | async-start | bytes 524288 | tf_op jit(solution)/shard_map/all_to_all | solution.py:333
  65.3 9.2 %collective-permute-start.5 = (f16[1040,128]{1,0:T(8,128)(2,1)S(1)}, f16[1040,128]{1,0:T(8,128)(2,1)S(1)}, u32[]{:S(2)}, u32[]{:S(2)}) collective-permute-start(f16[1040,128]{1,0:T(8,128)(2,1)S(1)} %convert_element_type.46), channel_id=1, source_target_pairs={{0,2},{2,0},{4,6},{6,4},{8,10},{10,8},{12,14},{14,12},{1,3},{3,1},... | collective-permute-start | bytes 798728 | tf_op jit(solution)/shard_map/ppermute | solution.py:320
  67.5 21.6 %collective-permute-start.6 = (f16[272,128]{1,0:T(8,128)(2,1)S(1)}, f16[272,128]{1,0:T(8,128)(2,1)S(1)}, u32[]{:S(2)}, u32[]{:S(2)}) collective-permute-start(f16[272,128]{1,0:T(8,128)(2,1)S(1)} %convert_element_type.47), channel_id=1, source_target_pairs={{0,1},{1,0},{2,3},{3,2},{4,5},{5,4},{6,7},{7,6},{8,9},{9,8},{10,11... | collective-permute-start | bytes 208904 | tf_op jit(solution)/shard_map/ppermute | solution.py:334
  75.4 10.1 %collective-permute-start.7 = (f16[528,128]{1,0:T(8,128)(2,1)S(1)}, f16[528,128]{1,0:T(8,128)(2,1)S(1)}, u32[]{:S(2)}, u32[]{:S(2)}) collective-permute-start(f16[528,128]{1,0:T(8,128)(2,1)S(1)} %pad_maximum_fusion.2), channel_id=1, source_target_pairs={{0,4},{2,6},{4,0},{6,2},{8,12},{10,14},{12,8},{14,10},{1,5},{3,7},... | collective-permute-start | bytes 405512 | tf_op jit(solution)/shard_map/ppermute | solution.py:264
  78.7 15.6 %all-to-all-start.2 = ((bf16[32,16,128]{2,1,0:T(8,128)(2,1)}), bf16[32,16,128]{2,1,0:T(8,128)(2,1)S(1)}, u32[]{:S(2)}, u32[]{:S(2)}) async-start(bf16[32,16,128]{2,1,0:T(8,128)(2,1)} %bitcast.20), calls=%async_computation.2 | async-start | bytes 262144 | tf_op jit(solution)/shard_map/all_to_all | solution.py:350
  85.6 15.0 %collective-permute-start.9 = (f16[272,128]{1,0:T(8,128)(2,1)S(1)}, f16[272,128]{1,0:T(8,128)(2,1)S(1)}, u32[]{:S(2)}, u32[]{:S(2)}) collective-permute-start(f16[272,128]{1,0:T(8,128)(2,1)S(1)} %pad_maximum_fusion.3), channel_id=1, source_target_pairs={{0,8},{2,10},{4,12},{6,14},{8,0},{10,2},{12,4},{14,6},{1,9},{3,11}... | collective-permute-start | bytes 208904 | tf_op jit(solution)/shard_map/ppermute | solution.py:345
  94.3 6.6 %collective-permute-start.8 = (bf16[16,2,16,128]{3,2,1,0:T(8,128)(2,1)S(1)}, bf16[16,2,16,128]{3,2,1,0:T(8,128)(2,1)S(1)}, u32[]{:S(2)}, u32[]{:S(2)}) collective-permute-start(bf16[16,2,16,128]{3,2,1,0:T(8,128)(2,1)S(1)} %bitcast.68), channel_id=1, source_target_pairs={{0,16},{16,0},{1,17},{17,1},{2,18},{18,2},{3,19},{19,3},{4,20},{20... | collective-permute-start | bytes 393224 | tf_op jit(solution)/shard_map/ppermute | solution.py:353

commit v4 on v3

--- a/solution.py
+++ b/solution.py
@@ -60,22 +60,21 @@
     dst[slot, row, 2] = jnp.where(lane == 127, 0.0, pltpu.roll(wide, 127, 1)).astype(BF)
 
 
-def data_kernel(place, wown, wgot, own, got, other, rim, keep, send, planes, peak):
+def data_kernel(place, wown, wgot, own, got, other, keep, send, planes, peak):
     j = place[0]
     zero = jnp.zeros((3, 32, 128), BF)
     for slot in range(4):
         planes[slot, 0] = zero
         planes[slot, 9] = zero
 
-    def fill(row, _):
-        for s in range(2):
-            put(planes, 1 + s, row + 1, jnp.concatenate([own[s, row], got[s, row]], axis=0))
+    def fill(row):
+        for s in range(3):
+            put(planes, s + j, row + 1, jnp.concatenate([own[s, row], got[s, row]], axis=0))
         near = jnp.concatenate([other[0, j, row], other[1, j, row]], axis=0)
         put(planes, 3 * (1 - j), row + 1, near)
-        put(planes, 3 * j, row + 1, jnp.concatenate([rim[0, row], rim[1, row]], axis=0))
-        return 0
-
-    lax.fori_loop(0, 8, fill, 0)
+
+    for step in range(8):
+        fill(step)
     peak[...] = jnp.zeros_like(peak)
     turned = iota((128, 128), 0) ^ (16 * place[1])
     pick = jnp.where(turned == iota((128, 128), 1), 1.0, 0.0).astype(BF)
@@ -95,7 +94,7 @@
         flat = planes[pl.ds(plane, 3), pl.ds(row, 3)].reshape(864, 128)
         return jnp.concatenate([flat, jnp.zeros((32, 128), BF)], axis=0)
 
-    def row_pair(step, _):
+    def row_pair(step):
         p, h = step // 4, 2 * (step % 4)
         rhs = jnp.concatenate([window(p, h), window(p, h + 1)], axis=1)
         res = jnp.dot(lhs, rhs, preferred_element_type=F32)
@@ -108,18 +107,18 @@
             out[rows] = res[16 * m : 16 * m + 16, 128:]
         sizes = jnp.maximum(jnp.abs(res[:, :128]), jnp.abs(res[:, 128:]))
         peak[...] = jnp.maximum(peak[...], jnp.max(sizes.reshape(16, 8, 128), axis=0))
-        return 0
-
-    lax.fori_loop(0, 8, row_pair, 0)
+
+    for step in range(8):
+        row_pair(step)
     size = size_of(peak[...])
     scale = jnp.exp2(14.0 - size)
 
-    def bring(step, _):
-        rows = pl.ds(pl.multiple_of(step * 64, 64), 64)
+    def bring(step):
+        rows = pl.ds(step * 64, 64)
         send[rows] = (send[rows].reshape(8, 8, 128) * scale).reshape(64, 128)
-        return 0
-
-    lax.fori_loop(0, 16, bring, 0)
+
+    for step in range(16):
+        bring(step)
     send[1024:1032] = size
     send[1032:1040] = size
 
@@ -132,18 +131,20 @@
     resp[...] = jnp.zeros_like(resp)
     half = pl.ds(pl.multiple_of(64 * j, 64), 64)
 
-    def fill(row, _):
+    def fill(row):
         for s in range(3):
             put(planes, 3 * j + s, row, vown[:, s, row].reshape(128, 128))
             put(planes, 3 * (1 - j) + s, row, vother[:, s, row].reshape(128, 128))
         for s in range(2):
-            cot[2 + 2 * j + s, row + 1] = jnp.concatenate([cown[s, row], cgot[s, row]], axis=0)
+            cot[2 + 2 * j + s, row + 1] = jnp.concatenate(
+                [cown[s + 1 - j, row], cgot[s + 1 - j, row]], axis=0
+            )
             cot[4 - 2 * j + s, row + 1] = jnp.concatenate(
                 [cother[0, s, row], cother[1, s, row]], axis=0
             )
-        return 0
-
-    lax.fori_loop(0, 8, fill, 0)
+
+    for step in range(8):
+        fill(step)
 
     weights = jnp.concatenate(
         [
@@ -156,7 +157,7 @@
         axis=0,
     )
 
-    def row_pair(step, _):
+    def row_pair(step):
         h = 2 * step
         for q in range(4):
             reach = [a for a in range(3) if 0 <= q - a < 2]
@@ -171,9 +172,9 @@
                     at = 96 * n + 32 * b
                     resp[q - a, h + 2 - b] += res[at : at + 32, :128]
                     resp[q - a, h + 3 - b] += res[at : at + 32, 128:]
-        return 0
-
-    lax.fori_loop(0, 4, row_pair, 0)
+
+    for step in range(4):
+        row_pair(step)
     peak = jnp.zeros((8, 128), F32)
     for p in range(2):
         for h in range(8):
@@ -281,42 +282,41 @@
     swap = [(0, 1), (1, 0)]
 
     fields = jnp.transpose(jnp.stack([volume, cotangent]), (0, 2, 3, 1, 4))
-    grad = fields[1]
     near = [(2 * i + 1, 2 * i + 2) for i in range(chips - 1)]
     near = near + [(t, s) for s, t in near]
 
-    def rim_of(value, axis):
-        return lax.dynamic_index_in_dim(value, core, axis, keepdims=False)
+    rims = lax.ppermute(
+        lax.dynamic_index_in_dim(fields, core, 1), ("xz", "co"), near
+    )
+    fields = jnp.where(
+        core == 0,
+        jnp.concatenate([rims, fields], axis=1),
+        jnp.concatenate([fields, rims], axis=1),
+    )
+    slab, grad = fields[0], fields[1]
 
     tap_blocks = jnp.transpose(filters, (1, 2, 3, 0, 4)).reshape(27, 16, 256)
     wown, wsend = call(
         pack_kernel, [jax.ShapeDtypeStruct((27, 16, 128), BF)] * 2, [place, tap_blocks]
     )
     pair = lax.ppermute(
-        jnp.concatenate([grad.reshape(256, 128), wsend.reshape(432, 128)]), "zh", swap
-    )
-    grad_got = pair[:256].reshape(2, 8, 16, 128)
-    wgot = pair[256:].reshape(27, 16, 128)
+        jnp.concatenate([grad.reshape(384, 128), wsend.reshape(432, 128)]), "zh", swap
+    )
+    grad_got = pair[:384].reshape(3, 8, 16, 128)
+    wgot = pair[384:].reshape(27, 16, 128)
     both = jnp.stack([grad, grad_got])
-    grad_other = lax.ppermute(both, "co", swap)
-    grad_rim = lax.ppermute(rim_of(both, 1), ("xz", "co"), near)
-
+    grad_other = lax.ppermute(jnp.where(core == 0, both[:, 1:], both[:, :2]), "co", swap)
+    vol = lax.all_to_all(jnp.broadcast_to(slab[None], (8, 3, 8, 16, 128)), "y", 0, 0)
+    vol, grad_other = lax.optimization_barrier((vol, grad_other))
+    vol_other = lax.ppermute(vol, "co", swap)
     data_keep, data_send = call(
         data_kernel,
         [jax.ShapeDtypeStruct((1024, 128), F32), jax.ShapeDtypeStruct((1040, 128), F32)],
-        [place, wown, wgot, grad, grad_got, grad_other, grad_rim],
+        [place, wown, wgot, grad, grad_got, grad_other],
         [pltpu.VMEM((4, 10, 3, 32, 128), BF), pltpu.VMEM((8, 128), F32)],
         micros=10,
     )
-    rim = lax.ppermute(rim_of(fields[0], 0), ("xz", "co"), near)[None]
-    slab = jnp.where(
-        core == 0,
-        jnp.concatenate([rim, fields[0]], axis=0),
-        jnp.concatenate([fields[0], rim], axis=0),
-    )
-    vol = lax.all_to_all(jnp.broadcast_to(slab[None], (8, 3, 8, 16, 128)), "y", 0, 0)
-    vol, data_keep, data_send = lax.optimization_barrier((vol, data_keep, data_send))
-    vol_other = lax.ppermute(vol, "co", swap)
+    vol_other, data_keep, data_send = lax.optimization_barrier((vol_other, data_keep, data_send))
     data_got = lax.ppermute(data_send.astype(F16), "y", [(i, i ^ 1) for i in range(8)])
     rkeep, rsend, taps = call(
         volume_kernel,

time: 104 us -> 100 us (0.962)
  waiting for transfers between devices: 26.7 us -> 15.9 us
  starting transfers between devices: 59.3 us -> 69.7 us
  Pallas kernels: 11.7 us -> 8.49 us
    all_to_all x1, waiting for transfers between devices: 10.7 us -> 3.61 us  [local(): lax.all_to_all(jnp.broadcast_to(slab[None], (8, 3, 8, 16, 128)), 'y', 0, 0)]
    ppermute x1, starting transfers between devices: 2.07 us -> 7.84 us  [local(): got = lax.ppermute(rsend.astype(F16), 'zh', swap)]
    ppermute x1, waiting for transfers between devices: 4.96 us -> 0.01 us  [local(): lax.ppermute(data_send.astype(F16), 'y', [(i, i ^ 1) for i in range(8)])]
    all_to_all x1, starting transfers between devices: 8.03 us -> 12.9 us  [local(): kernel = lax.all_to_all(taps.reshape(16, 32, 128), 'xz', 0, 0)]
    ppermute x4 -> x3, waiting for transfers between devices: 2.38 us -> 6.48 us  [the longest x1 3.27 us: local(): lax.ppermute(jnp.concatenate([grad.reshape(384, 128), wsend.reshape(432,...]
    ppermute x4 -> x3, starting transfers between devices: 20.7 us -> 17.1 us  [the longest x1 9.74 us: local(): lax.ppermute(jnp.concatenate([grad.reshape(384, 128), wsend.reshape(432,...]
    pallas_call x5, Pallas kernels: 11.7 us -> 8.49 us  [call(): pl.pallas_call(kernel, out_shape=out_shape, in_specs=[SMEM] + [VMEM] * (l...]
    all_to_all x1, starting transfers between devices: 6.23 us -> 8.39 us  [local(): kernel = lax.all_to_all(kernel, ('xz', 'zh'), 0, 0).reshape(16, 2, 16, 128)]
  transfers between devices with their start and end apart: 13 -> 12, of which waited for: 8 -> 7; matrix products, arithmetic and copies ran while one was open for 3% -> 2% of each run, Pallas kernels for 5% -> 3%
where the time goes in v4:
time: 100 us; the launch traced here: 99.6 us
  starting transfers between devices  69.7 us (70%)
  waiting for transfers between devices  15.9 us (16%)
  Pallas kernels  8.49 us (8%)
  local copies, waits for them, and re-layouts  4 us (4%)
    all_to_all x1, starting transfers between devices, local(): kernel = lax.all_to_all(taps.reshape(16, 32, 128), 'xz', 0, 0)  12.9 us
    ppermute x1, starting transfers between devices, local(): lax.ppermute(jnp.concatenate([grad.reshape(384, 128), wsend.reshape(432,...  9.74 us
    pallas_call x5, Pallas kernels, call(): pl.pallas_call(kernel, out_shape=out_shape, in_specs=[SMEM] + [VMEM] * (l...  8.49 us
    all_to_all x1, starting transfers between devices, local(): kernel = lax.all_to_all(kernel, ('xz', 'zh'), 0, 0).reshape(16, 2, 16, 128)  8.39 us
    ppermute x1, starting transfers between devices, local(): got = lax.ppermute(rsend.astype(F16), 'zh', swap)  7.84 us
    all_to_all x1, starting transfers between devices, local(): lax.all_to_all(jnp.broadcast_to(slab[None], (8, 3, 8, 16, 128)), 'y', 0, 0)  6.95 us
    ppermute x1, starting transfers between devices, local(): kernel_other = lax.ppermute(kernel, 'co', swap)  5.64 us
    ppermute x1, starting transfers between devices, local(): lax.ppermute(lax.dynamic_index_in_dim(fields, core, 1), ('xz', 'co'), near)  5.39 us
  transfers between devices with their start and end apart: 12, of which 7 were waited for; matrix products, arithmetic and copies ran while one was open for 2% of the time, Pallas kernels for 3%

profile of v4, /device:TPU:1, one launch (start us, length us, event | category | flops | bytes accessed | tf_op | source)
XLA Modules:
  0.0 99.6 jit_solution(5293296462648667138)
XLA Ops:
  0.6 0.9 copy_bitcast_fusion.2
  1.6 5.4 %collective-permute-start = (bf16[2,1,8,16,128]{4,3,2,1,0:T(8,128)(2,1)S(1)}, bf16[2,1,8,16,128]{4,3,2,1,0:T(8,128)(2,1)S(1)}, u32[]{:S(2)}, u32[]{:S(2)}) collective-permute-start(bf16[2,1,8,16,128]{4,3,2,1,0:T(8,128)(2,1)S(1)} %fusion.7), channel_id=1, source_target_pairs={{16,32},{48,64},{80,96},{112,128},{144,160},{176,192},{208,224},{2... | collective-permute-start | bytes 196616 | tf_op jit(solution)/shard_map/ppermute | solution.py:288
  7.0 1.9 %collective-permute-done = bf16[2,1,8,16,128]{4,3,2,1,0:T(8,128)(2,1)S(1)} collective-permute-done((bf16[2,1,8,16,128]{4,3,2,1,0:T(8,128)(2,1)S(1)}, bf16[2,1,8,16,128]{4,3,2,1,0:T(8,128)(2,1)S(1)}, u32[]{:S(2)}, u32[]{:S(2)}) %collective-permute-start) | collective-permute-done | bytes 65568 | tf_op jit(solution)/shard_map/ppermute | solution.py:288
  9.0 1.1 %broadcast_in_dim.30 = bf16[8,3,8,16,128]{4,3,2,1,0:T(8,128)(2,1)} broadcast(bf16[3,8,16,128]{3,2,1,0:T(8,128)(2,1)S(1)} %get-tuple-element.43), dimensions={1,2,3,4} | broadcast | bytes 884736 | tf_op jit(solution)/shard_map/broadcast_in_dim | solution.py:309
  10.0 0.0 copy-start
  10.0 7.0 %all-to-all-start = ((bf16[8,3,8,16,128]{4,3,2,1,0:T(8,128)(2,1)}), bf16[8,3,8,16,128]{4,3,2,1,0:T(8,128)(2,1)S(1)}, u32[]{:S(2)}, u32[]{:S(2)}) async-start(bf16[8,3,8,16,128]{4,3,2,1,0:T(8,128)(2,1)} %broadcast_in_dim.30), calls=%async_computation | async-start | bytes 1572864 | tf_op jit(solution)/shard_map/all_to_all | solution.py:309
  17.0 0.1 pad_add_fusion.place
  17.1 0.0 copy-done
  17.1 0.8 shard_map.58
  17.9 9.7 %collective-permute-start.1 = (bf16[816,128]{1,0:T(8,128)(2,1)S(1)}, bf16[816,128]{1,0:T(8,128)(2,1)S(1)}, u32[]{:S(2)}, u32[]{:S(2)}) collective-permute-start(bf16[816,128]{1,0:T(8,128)(2,1)S(1)} %pad_maximum_fusion), channel_id=1, source_target_pairs={{0,1},{1,0},{2,3},{3,2},{4,5},{5,4},{6,7},{7,6},{8,9},{9,8},{10,11... | collective-permute-start | bytes 626696 | tf_op jit(solution)/shard_map/ppermute | solution.py:302
  27.6 3.3 %collective-permute-done.1 = bf16[816,128]{1,0:T(8,128)(2,1)S(1)} collective-permute-done((bf16[816,128]{1,0:T(8,128)(2,1)S(1)}, bf16[816,128]{1,0:T(8,128)(2,1)S(1)}, u32[]{:S(2)}, u32[]{:S(2)}) %collective-permute-start.1) | collective-permute-done | bytes 208928 | tf_op jit(solution)/shard_map/ppermute | solution.py:302
  30.9 1.9 %collective-permute-start.2 = (bf16[2,2,8,16,128]{4,3,2,1,0:T(8,128)(2,1)S(1)}, bf16[2,2,8,16,128]{4,3,2,1,0:T(8,128)(2,1)S(1)}, u32[]{:S(2)}, u32[]{:S(2)}) collective-permute-start(bf16[2,2,8,16,128]{4,3,2,1,0:T(8,128)(2,1)S(1)} %fusion.2), channel_id=1, source_target_pairs={{0,16},{16,0},{1,17},{17,1},{2,18},{18,2},{3,19},{19,3},{4,20},{20... | collective-permute-start | bytes 393224 | tf_op jit(solution)/shard_map/ppermute | solution.py:308
  32.9 1.3 %collective-permute-done.2.other.cother = bf16[2,2,8,16,128]{4,3,2,1,0:T(8,128)(2,1)S(1)} collective-permute-done((bf16[2,2,8,16,128]{4,3,2,1,0:T(8,128)(2,1)S(1)}, bf16[2,2,8,16,128]{4,3,2,1,0:T(8,128)(2,1)S(1)}, u32[]{:S(2)}, u32[]{:S(2)}) %collective-permute-start.2) | collective-permute-done | bytes 131104 | tf_op jit(solution)/shard_map/ppermute | solution.py:308
  34.2 3.6 %all-to-all-done.vown = bf16[8,3,8,16,128]{4,3,2,1,0:T(8,128)(2,1)S(1)} async-done(((bf16[8,3,8,16,128]{4,3,2,1,0:T(8,128)(2,1)}), bf16[8,3,8,16,128]{4,3,2,1,0:T(8,128)(2,1)S(1)}, u32[]{:S(2)}, u32[]{:S(2)}) %all-to-all-start) | async-done | bytes 786464 | tf_op jit(solution)/shard_map/all_to_all | solution.py:309
  37.8 1.9 %collective-permute-start.3 = (bf16[8,3,8,16,128]{4,3,2,1,0:T(8,128)(2,1)S(1)}, bf16[8,3,8,16,128]{4,3,2,1,0:T(8,128)(2,1)S(1)}, u32[]{:S(2)}, u32[]{:S(2)}) collective-permute-start(bf16[8,3,8,16,128]{4,3,2,1,0:T(8,128)(2,1)S(1)} %all-to-all-done.vown), channel_id=1, source_target_pairs={{0,16},{16,0},{1,17},{17,1},{2,18},{18,2},{3,19},{19,3},{4,20},{20... | collective-permute-start | bytes 2359304 | tf_op jit(solution)/shard_map/ppermute | solution.py:311
  39.7 1.6 %shard_map.59 = (f32[1024,128]{1,0:T(8,128)S(1)}, f32[1040,128]{1,0:T(8,128)S(1)}) custom-call(s32[3]{0:T(128)S(1)} %pad_add_fusion.place, bf16[27,16,128]{2,1,0:T(8,128)(2,1)S(1)} %get-tuple-element.21.wown, bf16[27,16,128]{2,1,0:T(8,128)(2,1)S(1)} %bitcast.66, bf16[3,8,16,128]{3,2,1,0:T(8,128)(2,1)S(1)} %get-tuple-element.42.own.cown, ...), custom_call_target="tpu_custom_call" | custom-call | flops 10000000000 | bytes 262144 | tf_op jit(solution)/shard_map/pallas_call | solution.py:22
  41.3 0.6 collective-permute-done.3.vother
  41.9 3.8 %shard_map.60 = (f32[256,128]{1,0:T(8,128)S(1)}, f32[272,128]{1,0:T(8,128)S(1)}, f32[512,128]{1,0:T(8,128)}) custom-call(s32[3]{0:T(128)S(1)} %pad_add_fusion.place, bf16[27,16,128]{2,1,0:T(8,128)(2,1)S(1)} %get-tuple-element.21.wown, bf16[27,16,128]{2,1,0:T(8,128)(2,1)S(1)} %bitcast.67, bf16[8,3,8,16,128]{4,3,2,1,0:T(8,128)(2,1)S(1)} %all-to-all-done.vown, ...), custom_call_target="tpu_custom_call" | custom-call | flops 8000000000 | bytes 262144 | tf_op jit(solution)/shard_map/pallas_call | solution.py:22
  45.8 12.9 %all-to-all-start.1 = ((f32[16,32,128]{2,1,0:T(8,128)}), f32[16,32,128]{2,1,0:T(8,128)S(1)}, u32[]{:S(2)}, u32[]{:S(2)}) async-start(f32[16,32,128]{2,1,0:T(8,128)} %bitcast.16), calls=%async_computation.1 | async-start | bytes 524288 | tf_op jit(solution)/shard_map/all_to_all | solution.py:333
  58.7 2.1 %collective-permute-start.4 = (f16[1040,128]{1,0:T(8,128)(2,1)S(1)}, f16[1040,128]{1,0:T(8,128)(2,1)S(1)}, u32[]{:S(2)}, u32[]{:S(2)}) collective-permute-start(f16[1040,128]{1,0:T(8,128)(2,1)S(1)} %convert_element_type.46), channel_id=1, source_target_pairs={{0,2},{2,0},{4,6},{6,4},{8,10},{10,8},{12,14},{14,12},{1,3},{3,1},... | collective-permute-start | bytes 798728 | tf_op jit(solution)/shard_map/ppermute | solution.py:320
  60.8 7.8 %collective-permute-start.5 = (f16[272,128]{1,0:T(8,128)(2,1)S(1)}, f16[272,128]{1,0:T(8,128)(2,1)S(1)}, u32[]{:S(2)}, u32[]{:S(2)}) collective-permute-start(f16[272,128]{1,0:T(8,128)(2,1)S(1)} %convert_element_type.47), channel_id=1, source_target_pairs={{0,1},{1,0},{2,3},{3,2},{4,5},{5,4},{6,7},{7,6},{8,9},{9,8},{10,11... | collective-permute-start | bytes 208904 | tf_op jit(solution)/shard_map/ppermute | solution.py:334
  68.7 0.0 collective-permute-done.4
  68.7 0.0 all-to-all-done.1.parts
  68.7 0.6 shard_map.61
  69.3 0.1 multiply_add_fusion
  69.5 2.7 %collective-permute-start.6 = (f16[528,128]{1,0:T(8,128)(2,1)S(1)}, f16[528,128]{1,0:T(8,128)(2,1)S(1)}, u32[]{:S(2)}, u32[]{:S(2)}) collective-permute-start(f16[528,128]{1,0:T(8,128)(2,1)S(1)} %pad_maximum_fusion.2), channel_id=1, source_target_pairs={{0,4},{2,6},{4,0},{6,2},{8,12},{10,14},{12,8},{14,10},{1,5},{3,7},... | collective-permute-start | bytes 405512 | tf_op jit(solution)/shard_map/ppermute | solution.py:265
  72.2 0.7 broadcast_in_dim.31
  72.8 8.4 %all-to-all-start.2 = ((bf16[32,16,128]{2,1,0:T(8,128)(2,1)}), bf16[32,16,128]{2,1,0:T(8,128)(2,1)S(1)}, u32[]{:S(2)}, u32[]{:S(2)}) async-start(bf16[32,16,128]{2,1,0:T(8,128)(2,1)} %bitcast.18), calls=%async_computation.2 | async-start | bytes 262144 | tf_op jit(solution)/shard_map/all_to_all | solution.py:350
  81.2 0.0 collective-permute-done.6
  81.4 4.3 %collective-permute-start.8 = (f16[272,128]{1,0:T(8,128)(2,1)S(1)}, f16[272,128]{1,0:T(8,128)(2,1)S(1)}, u32[]{:S(2)}, u32[]{:S(2)}) collective-permute-start(f16[272,128]{1,0:T(8,128)(2,1)S(1)} %pad_maximum_fusion.4), channel_id=1, source_target_pairs={{0,8},{2,10},{4,12},{6,14},{8,0},{10,2},{12,4},{14,6},{1,9},{3,11}... | collective-permute-start | bytes 208904 | tf_op jit(solution)/shard_map/ppermute | solution.py:345
  85.7 0.0 collective-permute-done.5
  85.7 4.9 %all-to-all-done.2 = bf16[32,16,128]{2,1,0:T(8,128)(2,1)S(1)} async-done(((bf16[32,16,128]{2,1,0:T(8,128)(2,1)}), bf16[32,16,128]{2,1,0:T(8,128)(2,1)S(1)}, u32[]{:S(2)}, u32[]{:S(2)}) %all-to-all-start.2) | async-done | bytes 131104 | tf_op jit(solution)/shard_map/all_to_all | solution.py:350
  90.6 5.6 %collective-permute-start.7 = (bf16[16,2,16,128]{3,2,1,0:T(8,128)(2,1)S(1)}, bf16[16,2,16,128]{3,2,1,0:T(8,128)(2,1)S(1)}, u32[]{:S(2)}, u32[]{:S(2)}) collective-permute-start(bf16[16,2,16,128]{3,2,1,0:T(8,128)(2,1)S(1)} %bitcast.64), channel_id=1, source_target_pairs={{0,16},{16,0},{1,17},{17,1},{2,18},{18,2},{3,19},{19,3},{4,20},{20... | collective-permute-start | bytes 393224 | tf_op jit(solution)/shard_map/ppermute | solution.py:353
  96.3 0.6 copy.15
  96.9 0.0 collective-permute-done.8
  96.9 0.3 collective-permute-done.7.other
  97.2 1.7 %shard_map.62 = bf16[27,16,256]{2,1,0:T(8,128)(2,1)} custom-call(s32[3]{0:T(128)S(1)} %pad_add_fusion.place, bf16[16,2,16,128]{3,2,1,0:T(8,128)(2,1)S(1)} %bitcast.65, bf16[16,2,16,128]{3,2,1,0:T(8,128)(2,1)S(1)} %collective-permute-done.7.other), custom_call_target="tpu_custom_call" | custom-call | flops 1000000000 | bytes 262144 | tf_op jit(solution)/shard_map/pallas_call | solution.py:22
  98.9 0.6 copy.14
  (26 shorter events, 0.5 us)
Async XLA Ops:
  1.6 7.3 %collective-permute-start = (bf16[2,1,8,16,128]{4,3,2,1,0:T(8,128)(2,1)S(1)}, bf16[2,1,8,16,128]{4,3,2,1,0:T(8,128)(2,1)S(1)}, u32[]{:S(2)}, u32[]{:S(2)}) collective-permute-start(bf16[2,1,8,16,128]{4,3,2,1,0:T(8,128)(2,1)S(1)} %fusion.7), channel_id=1, source_target_pairs={{16,32},{48,64},{80,96},{112,128},{144,160},{176,192},{208,224},{2... | collective-permute-start | bytes 196616 | tf_op jit(solution)/shard_map/ppermute | solution.py:288
  10.0 7.0 %copy-start = (bf16[16,3,3,3,256]{4,0,3,2,1:T(8,128)(2,1)S(1)}, bf16[16,3,3,3,256]{4,0,3,2,1:T(8,128)(2,1)}, u32[]{:S(2)}) copy-start(bf16[16,3,3,3,256]{4,0,3,2,1:T(8,128)(2,1)} %param.4) | copy-start | bytes 663556
  10.0 27.7 %all-to-all-start = ((bf16[8,3,8,16,128]{4,3,2,1,0:T(8,128)(2,1)}), bf16[8,3,8,16,128]{4,3,2,1,0:T(8,128)(2,1)S(1)}, u32[]{:S(2)}, u32[]{:S(2)}) async-start(bf16[8,3,8,16,128]{4,3,2,1,0:T(8,128)(2,1)} %broadcast_in_dim.30), calls=%async_computation | async-start | bytes 1572864 | tf_op jit(solution)/shard_map/all_to_all | solution.py:309
  17.9 13.0 %collective-permute-start.1 = (bf16[816,128]{1,0:T(8,128)(2,1)S(1)}, bf16[816,128]{1,0:T(8,128)(2,1)S(1)}, u32[]{:S(2)}, u32[]{:S(2)}) collective-permute-start(bf16[816,128]{1,0:T(8,128)(2,1)S(1)} %pad_maximum_fusion), channel_id=1, source_target_pairs={{0,1},{1,0},{2,3},{3,2},{4,5},{5,4},{6,7},{7,6},{8,9},{9,8},{10,11... | collective-permute-start | bytes 626696 | tf_op jit(solution)/shard_map/ppermute | solution.py:302
  30.9 3.2 %collective-permute-start.2 = (bf16[2,2,8,16,128]{4,3,2,1,0:T(8,128)(2,1)S(1)}, bf16[2,2,8,16,128]{4,3,2,1,0:T(8,128)(2,1)S(1)}, u32[]{:S(2)}, u32[]{:S(2)}) collective-permute-start(bf16[2,2,8,16,128]{4,3,2,1,0:T(8,128)(2,1)S(1)} %fusion.2), channel_id=1, source_target_pairs={{0,16},{16,0},{1,17},{17,1},{2,18},{18,2},{3,19},{19,3},{4,20},{20... | collective-permute-start | bytes 393224 | tf_op jit(solution)/shard_map/ppermute | solution.py:308
  37.8 4.2 %collective-permute-start.3 = (bf16[8,3,8,16,128]{4,3,2,1,0:T(8,128)(2,1)S(1)}, bf16[8,3,8,16,128]{4,3,2,1,0:T(8,128)(2,1)S(1)}, u32[]{:S(2)}, u32[]{:S(2)}) collective-permute-start(bf16[8,3,8,16,128]{4,3,2,1,0:T(8,128)(2,1)S(1)} %all-to-all-done.vown), channel_id=1, source_target_pairs={{0,16},{16,0},{1,17},{17,1},{2,18},{18,2},{3,19},{19,3},{4,20},{20... | collective-permute-start | bytes 2359304 | tf_op jit(solution)/shard_map/ppermute | solution.py:311
  45.8 22.9 %all-to-all-start.1 = ((f32[16,32,128]{2,1,0:T(8,128)}), f32[16,32,128]{2,1,0:T(8,128)S(1)}, u32[]{:S(2)}, u32[]{:S(2)}) async-start(f32[16,32,128]{2,1,0:T(8,128)} %bitcast.16), calls=%async_computation.1 | async-start | bytes 524288 | tf_op jit(solution)/shard_map/all_to_all | solution.py:333
  58.7 10.0 %collective-permute-start.4 = (f16[1040,128]{1,0:T(8,128)(2,1)S(1)}, f16[1040,128]{1,0:T(8,128)(2,1)S(1)}, u32[]{:S(2)}, u32[]{:S(2)}) collective-permute-start(f16[1040,128]{1,0:T(8,128)(2,1)S(1)} %convert_element_type.46), channel_id=1, source_target_pairs={{0,2},{2,0},{4,6},{6,4},{8,10},{10,8},{12,14},{14,12},{1,3},{3,1},... | collective-permute-start | bytes 798728 | tf_op jit(solution)/shard_map/ppermute | solution.py:320
  60.8 24.9 %collective-permute-start.5 = (f16[272,128]{1,0:T(8,128)(2,1)S(1)}, f16[272,128]{1,0:T(8,128)(2,1)S(1)}, u32[]{:S(2)}, u32[]{:S(2)}) collective-permute-start(f16[272,128]{1,0:T(8,128)(2,1)S(1)} %convert_element_type.47), channel_id=1, source_target_pairs={{0,1},{1,0},{2,3},{3,2},{4,5},{5,4},{6,7},{7,6},{8,9},{9,8},{10,11... | collective-permute-start | bytes 208904 | tf_op jit(solution)/shard_map/ppermute | solution.py:334
  69.5 11.8 %collective-permute-start.6 = (f16[528,128]{1,0:T(8,128)(2,1)S(1)}, f16[528,128]{1,0:T(8,128)(2,1)S(1)}, u32[]{:S(2)}, u32[]{:S(2)}) collective-permute-start(f16[528,128]{1,0:T(8,128)(2,1)S(1)} %pad_maximum_fusion.2), channel_id=1, source_target_pairs={{0,4},{2,6},{4,0},{6,2},{8,12},{10,14},{12,8},{14,10},{1,5},{3,7},... | collective-permute-start | bytes 405512 | tf_op jit(solution)/shard_map/ppermute | solution.py:265
  72.8 17.8 %all-to-all-start.2 = ((bf16[32,16,128]{2,1,0:T(8,128)(2,1)}), bf16[32,16,128]{2,1,0:T(8,128)(2,1)S(1)}, u32[]{:S(2)}, u32[]{:S(2)}) async-start(bf16[32,16,128]{2,1,0:T(8,128)(2,1)} %bitcast.18), calls=%async_computation.2 | async-start | bytes 262144 | tf_op jit(solution)/shard_map/all_to_all | solution.py:350
  81.4 15.5 %collective-permute-start.8 = (f16[272,128]{1,0:T(8,128)(2,1)S(1)}, f16[272,128]{1,0:T(8,128)(2,1)S(1)}, u32[]{:S(2)}, u32[]{:S(2)}) collective-permute-start(f16[272,128]{1,0:T(8,128)(2,1)S(1)} %pad_maximum_fusion.4), channel_id=1, source_target_pairs={{0,8},{2,10},{4,12},{6,14},{8,0},{10,2},{12,4},{14,6},{1,9},{3,11}... | collective-permute-start | bytes 208904 | tf_op jit(solution)/shard_map/ppermute | solution.py:345
  90.6 6.6 %collective-permute-start.7 = (bf16[16,2,16,128]{3,2,1,0:T(8,128)(2,1)S(1)}, bf16[16,2,16,128]{3,2,1,0:T(8,128)(2,1)S(1)}, u32[]{:S(2)}, u32[]{:S(2)}) collective-permute-start(bf16[16,2,16,128]{3,2,1,0:T(8,128)(2,1)S(1)} %bitcast.64), channel_id=1, source_target_pairs={{0,16},{16,0},{1,17},{17,1},{2,18},{18,2},{3,19},{19,3},{4,20},{20... | collective-permute-start | bytes 393224 | tf_op jit(solution)/shard_map/ppermute | solution.py:353

commit v5 on v4

--- a/solution.py
+++ b/solution.py
@@ -98,12 +98,11 @@
         p, h = step // 4, 2 * (step % 4)
         rhs = jnp.concatenate([window(p, h), window(p, h + 1)], axis=1)
         res = jnp.dot(lhs, rhs, preferred_element_type=F32)
-        at = (p * 8 + h) * 16
         for m in range(8):
             out = send if m % 2 else keep
-            rows = pl.ds(m // 2 * 256 + at, 16)
+            rows = pl.ds(m // 2 * 256 + p * 8 + h, 16, stride=16)
             out[rows] = res[16 * m : 16 * m + 16, :128]
-            rows = pl.ds(m // 2 * 256 + at + 16, 16)
+            rows = pl.ds(m // 2 * 256 + p * 8 + h + 1, 16, stride=16)
             out[rows] = res[16 * m : 16 * m + 16, 128:]
         sizes = jnp.maximum(jnp.abs(res[:, :128]), jnp.abs(res[:, 128:]))
         peak[...] = jnp.maximum(peak[...], jnp.max(sizes.reshape(16, 8, 128), axis=0))
@@ -353,14 +352,14 @@
     kernel_other = lax.ppermute(kernel, "co", swap)
     kernel_other, data_got = lax.optimization_barrier((kernel_other, data_got))
     data, power = merge(data_keep, data_send, data_got)
-    data = data.reshape(2, 8, 16, 128)
+    data = data.reshape(16, 2, 8, 128)
     placed = call(
         place_kernel, jax.ShapeDtypeStruct((27, 16, 256), BF), [place, kernel, kernel_other]
     )
     order = (2, 0, 1, 3)
     return (
         jnp.transpose(response.astype(BF), order),
-        jnp.transpose(data.astype(BF), order),
+        data.astype(BF),
         jnp.transpose(placed.reshape(3, 3, 3, 16, 256), (3, 0, 1, 2, 4)),
     )
 

time: 100 us -> 100 us (level)
  no operation moved by 1% of the time
where the time goes in v5:
time: 100 us; the launch traced here: 99.6 us
  starting transfers between devices  69.7 us (70%)
  waiting for transfers between devices  15.7 us (16%)
  Pallas kernels  8.65 us (9%)
  local copies, waits for them, and re-layouts  3.36 us (3%)
  other arithmetic  1.2 us (1%)
    all_to_all x1, starting transfers between devices, local(): kernel = lax.all_to_all(taps.reshape(16, 32, 128), 'xz', 0, 0)  12.9 us
    ppermute x1, starting transfers between devices, local(): lax.ppermute(jnp.concatenate([grad.reshape(384, 128), wsend.reshape(432,...  9.74 us
    pallas_call x5, Pallas kernels, call(): pl.pallas_call(kernel, out_shape=out_shape, in_specs=[SMEM] + [VMEM] * (l...  8.65 us
    all_to_all x1, starting transfers between devices, local(): kernel = lax.all_to_all(kernel, ('xz', 'zh'), 0, 0).reshape(16, 2, 16, 128)  8.39 us
    ppermute x1, starting transfers between devices, local(): got = lax.ppermute(rsend.astype(F16), 'zh', swap)  7.84 us
    all_to_all x1, starting transfers between devices, local(): lax.all_to_all(jnp.broadcast_to(slab[None], (8, 3, 8, 16, 128)), 'y', 0, 0)  6.95 us
    ppermute x1, starting transfers between devices, local(): kernel_other = lax.ppermute(kernel, 'co', swap)  5.64 us
    ppermute x1, starting transfers between devices, local(): lax.ppermute(lax.dynamic_index_in_dim(fields, core, 1), ('xz', 'co'), near)  5.39 us
  transfers between devices with their start and end apart: 12, of which 7 were waited for; matrix products, arithmetic and copies ran while one was open for 2% of the time, Pallas kernels for 3%

profile of v5, /device:TPU:1, one launch (start us, length us, event | category | flops | bytes accessed | tf_op | source)
XLA Modules:
  0.0 99.6 jit_solution(14481050053826103318)
XLA Ops:
  0.6 0.9 copy_bitcast_fusion.1
  1.6 5.4 %collective-permute-start = (bf16[2,1,8,16,128]{4,3,2,1,0:T(8,128)(2,1)S(1)}, bf16[2,1,8,16,128]{4,3,2,1,0:T(8,128)(2,1)S(1)}, u32[]{:S(2)}, u32[]{:S(2)}) collective-permute-start(bf16[2,1,8,16,128]{4,3,2,1,0:T(8,128)(2,1)S(1)} %fusion.7), channel_id=1, source_target_pairs={{16,32},{48,64},{80,96},{112,128},{144,160},{176,192},{208,224},{2... | collective-permute-start | bytes 196616 | tf_op jit(solution)/shard_map/ppermute | solution.py:287
  7.0 1.9 %collective-permute-done = bf16[2,1,8,16,128]{4,3,2,1,0:T(8,128)(2,1)S(1)} collective-permute-done((bf16[2,1,8,16,128]{4,3,2,1,0:T(8,128)(2,1)S(1)}, bf16[2,1,8,16,128]{4,3,2,1,0:T(8,128)(2,1)S(1)}, u32[]{:S(2)}, u32[]{:S(2)}) %collective-permute-start) | collective-permute-done | bytes 65568 | tf_op jit(solution)/shard_map/ppermute | solution.py:287
  9.0 1.1 %broadcast_in_dim.30 = bf16[8,3,8,16,128]{4,3,2,1,0:T(8,128)(2,1)} broadcast(bf16[3,8,16,128]{3,2,1,0:T(8,128)(2,1)S(1)} %get-tuple-element.43), dimensions={1,2,3,4} | broadcast | bytes 884736 | tf_op jit(solution)/shard_map/broadcast_in_dim | solution.py:308
  10.0 0.0 copy-start
  10.0 7.0 %all-to-all-start = ((bf16[8,3,8,16,128]{4,3,2,1,0:T(8,128)(2,1)}), bf16[8,3,8,16,128]{4,3,2,1,0:T(8,128)(2,1)S(1)}, u32[]{:S(2)}, u32[]{:S(2)}) async-start(bf16[8,3,8,16,128]{4,3,2,1,0:T(8,128)(2,1)} %broadcast_in_dim.30), calls=%async_computation | async-start | bytes 1572864 | tf_op jit(solution)/shard_map/all_to_all | solution.py:308
  17.0 0.1 pad_add_fusion.place
  17.1 0.0 copy-done
  17.1 0.8 shard_map.58
  17.9 9.7 %collective-permute-start.1 = (bf16[816,128]{1,0:T(8,128)(2,1)S(1)}, bf16[816,128]{1,0:T(8,128)(2,1)S(1)}, u32[]{:S(2)}, u32[]{:S(2)}) collective-permute-start(bf16[816,128]{1,0:T(8,128)(2,1)S(1)} %pad_maximum_fusion), channel_id=1, source_target_pairs={{0,1},{1,0},{2,3},{3,2},{4,5},{5,4},{6,7},{7,6},{8,9},{9,8},{10,11... | collective-permute-start | bytes 626696 | tf_op jit(solution)/shard_map/ppermute | solution.py:301
  27.6 3.3 %collective-permute-done.1 = bf16[816,128]{1,0:T(8,128)(2,1)S(1)} collective-permute-done((bf16[816,128]{1,0:T(8,128)(2,1)S(1)}, bf16[816,128]{1,0:T(8,128)(2,1)S(1)}, u32[]{:S(2)}, u32[]{:S(2)}) %collective-permute-start.1) | collective-permute-done | bytes 208928 | tf_op jit(solution)/shard_map/ppermute | solution.py:301
  30.9 1.9 %collective-permute-start.2 = (bf16[2,2,8,16,128]{4,3,2,1,0:T(8,128)(2,1)S(1)}, bf16[2,2,8,16,128]{4,3,2,1,0:T(8,128)(2,1)S(1)}, u32[]{:S(2)}, u32[]{:S(2)}) collective-permute-start(bf16[2,2,8,16,128]{4,3,2,1,0:T(8,128)(2,1)S(1)} %fusion.2), channel_id=1, source_target_pairs={{0,16},{16,0},{1,17},{17,1},{2,18},{18,2},{3,19},{19,3},{4,20},{20... | collective-permute-start | bytes 393224 | tf_op jit(solution)/shard_map/ppermute | solution.py:307
  32.9 1.3 %collective-permute-done.2.other.cother = bf16[2,2,8,16,128]{4,3,2,1,0:T(8,128)(2,1)S(1)} collective-permute-done((bf16[2,2,8,16,128]{4,3,2,1,0:T(8,128)(2,1)S(1)}, bf16[2,2,8,16,128]{4,3,2,1,0:T(8,128)(2,1)S(1)}, u32[]{:S(2)}, u32[]{:S(2)}) %collective-permute-start.2) | collective-permute-done | bytes 131104 | tf_op jit(solution)/shard_map/ppermute | solution.py:307
  34.2 3.6 %all-to-all-done.vown = bf16[8,3,8,16,128]{4,3,2,1,0:T(8,128)(2,1)S(1)} async-done(((bf16[8,3,8,16,128]{4,3,2,1,0:T(8,128)(2,1)}), bf16[8,3,8,16,128]{4,3,2,1,0:T(8,128)(2,1)S(1)}, u32[]{:S(2)}, u32[]{:S(2)}) %all-to-all-start) | async-done | bytes 786464 | tf_op jit(solution)/shard_map/all_to_all | solution.py:308
  37.8 1.9 %collective-permute-start.3 = (bf16[8,3,8,16,128]{4,3,2,1,0:T(8,128)(2,1)S(1)}, bf16[8,3,8,16,128]{4,3,2,1,0:T(8,128)(2,1)S(1)}, u32[]{:S(2)}, u32[]{:S(2)}) collective-permute-start(bf16[8,3,8,16,128]{4,3,2,1,0:T(8,128)(2,1)S(1)} %all-to-all-done.vown), channel_id=1, source_target_pairs={{0,16},{16,0},{1,17},{17,1},{2,18},{18,2},{3,19},{19,3},{4,20},{20... | collective-permute-start | bytes 2359304 | tf_op jit(solution)/shard_map/ppermute | solution.py:310
  39.7 1.8 %shard_map.59 = (f32[1024,128]{1,0:T(8,128)S(1)}, f32[1040,128]{1,0:T(8,128)S(1)}) custom-call(s32[3]{0:T(128)S(1)} %pad_add_fusion.place, bf16[27,16,128]{2,1,0:T(8,128)(2,1)S(1)} %get-tuple-element.21.wown, bf16[27,16,128]{2,1,0:T(8,128)(2,1)S(1)} %bitcast.63, bf16[3,8,16,128]{3,2,1,0:T(8,128)(2,1)S(1)} %get-tuple-element.42.own.cown, ...), custom_call_target="tpu_custom_call" | custom-call | flops 10000000000 | bytes 262144 | tf_op jit(solution)/shard_map/pallas_call | solution.py:22
  41.5 0.4 collective-permute-done.3.vother
  41.9 3.8 %shard_map.60 = (f32[256,128]{1,0:T(8,128)S(1)}, f32[272,128]{1,0:T(8,128)S(1)}, f32[512,128]{1,0:T(8,128)}) custom-call(s32[3]{0:T(128)S(1)} %pad_add_fusion.place, bf16[27,16,128]{2,1,0:T(8,128)(2,1)S(1)} %get-tuple-element.21.wown, bf16[27,16,128]{2,1,0:T(8,128)(2,1)S(1)} %bitcast.64, bf16[8,3,8,16,128]{4,3,2,1,0:T(8,128)(2,1)S(1)} %all-to-all-done.vown, ...), custom_call_target="tpu_custom_call" | custom-call | flops 8000000000 | bytes 262144 | tf_op jit(solution)/shard_map/pallas_call | solution.py:22
  45.8 12.9 %all-to-all-start.1 = ((f32[16,32,128]{2,1,0:T(8,128)}), f32[16,32,128]{2,1,0:T(8,128)S(1)}, u32[]{:S(2)}, u32[]{:S(2)}) async-start(f32[16,32,128]{2,1,0:T(8,128)} %bitcast.16), calls=%async_computation.1 | async-start | bytes 524288 | tf_op jit(solution)/shard_map/all_to_all | solution.py:332
  58.7 2.1 %collective-permute-start.4 = (f16[1040,128]{1,0:T(8,128)(2,1)S(1)}, f16[1040,128]{1,0:T(8,128)(2,1)S(1)}, u32[]{:S(2)}, u32[]{:S(2)}) collective-permute-start(f16[1040,128]{1,0:T(8,128)(2,1)S(1)} %convert_element_type.46), channel_id=1, source_target_pairs={{0,2},{2,0},{4,6},{6,4},{8,10},{10,8},{12,14},{14,12},{1,3},{3,1},... | collective-permute-start | bytes 798728 | tf_op jit(solution)/shard_map/ppermute | solution.py:319
  60.8 7.8 %collective-permute-start.5 = (f16[272,128]{1,0:T(8,128)(2,1)S(1)}, f16[272,128]{1,0:T(8,128)(2,1)S(1)}, u32[]{:S(2)}, u32[]{:S(2)}) collective-permute-start(f16[272,128]{1,0:T(8,128)(2,1)S(1)} %convert_element_type.47), channel_id=1, source_target_pairs={{0,1},{1,0},{2,3},{3,2},{4,5},{5,4},{6,7},{7,6},{8,9},{9,8},{10,11... | collective-permute-start | bytes 208904 | tf_op jit(solution)/shard_map/ppermute | solution.py:333
  68.7 0.0 collective-permute-done.4
  68.7 0.0 all-to-all-done.1.parts
  68.7 0.6 shard_map.61
  69.3 0.1 multiply_add_fusion
  69.5 2.7 %collective-permute-start.6 = (f16[528,128]{1,0:T(8,128)(2,1)S(1)}, f16[528,128]{1,0:T(8,128)(2,1)S(1)}, u32[]{:S(2)}, u32[]{:S(2)}) collective-permute-start(f16[528,128]{1,0:T(8,128)(2,1)S(1)} %pad_maximum_fusion.2), channel_id=1, source_target_pairs={{0,4},{2,6},{4,0},{6,2},{8,12},{10,14},{12,8},{14,10},{1,5},{3,7},... | collective-permute-start | bytes 405512 | tf_op jit(solution)/shard_map/ppermute | solution.py:264
  72.2 0.7 broadcast_in_dim.31
  72.8 8.4 %all-to-all-start.2 = ((bf16[32,16,128]{2,1,0:T(8,128)(2,1)}), bf16[32,16,128]{2,1,0:T(8,128)(2,1)S(1)}, u32[]{:S(2)}, u32[]{:S(2)}) async-start(bf16[32,16,128]{2,1,0:T(8,128)(2,1)} %bitcast.18), calls=%async_computation.2 | async-start | bytes 262144 | tf_op jit(solution)/shard_map/all_to_all | solution.py:349
  81.2 0.0 collective-permute-done.6
  81.4 4.3 %collective-permute-start.8 = (f16[272,128]{1,0:T(8,128)(2,1)S(1)}, f16[272,128]{1,0:T(8,128)(2,1)S(1)}, u32[]{:S(2)}, u32[]{:S(2)}) collective-permute-start(f16[272,128]{1,0:T(8,128)(2,1)S(1)} %pad_maximum_fusion.4), channel_id=1, source_target_pairs={{0,8},{2,10},{4,12},{6,14},{8,0},{10,2},{12,4},{14,6},{1,9},{3,11}... | collective-permute-start | bytes 208904 | tf_op jit(solution)/shard_map/ppermute | solution.py:344
  85.7 0.0 collective-permute-done.5
  85.7 4.9 %all-to-all-done.2 = bf16[32,16,128]{2,1,0:T(8,128)(2,1)S(1)} async-done(((bf16[32,16,128]{2,1,0:T(8,128)(2,1)}), bf16[32,16,128]{2,1,0:T(8,128)(2,1)S(1)}, u32[]{:S(2)}, u32[]{:S(2)}) %all-to-all-start.2) | async-done | bytes 131104 | tf_op jit(solution)/shard_map/all_to_all | solution.py:349
  90.6 5.6 %collective-permute-start.7 = (bf16[16,2,16,128]{3,2,1,0:T(8,128)(2,1)S(1)}, bf16[16,2,16,128]{3,2,1,0:T(8,128)(2,1)S(1)}, u32[]{:S(2)}, u32[]{:S(2)}) collective-permute-start(bf16[16,2,16,128]{3,2,1,0:T(8,128)(2,1)S(1)} %bitcast.61), channel_id=1, source_target_pairs={{0,16},{16,0},{1,17},{17,1},{2,18},{18,2},{3,19},{19,3},{4,20},{20... | collective-permute-start | bytes 393224 | tf_op jit(solution)/shard_map/ppermute | solution.py:352
  96.3 0.6 copy.12
  96.9 0.0 collective-permute-done.8
  96.9 0.3 collective-permute-done.7.other
  97.2 1.7 %shard_map.62 = bf16[27,16,256]{2,1,0:T(8,128)(2,1)} custom-call(s32[3]{0:T(128)S(1)} %pad_add_fusion.place, bf16[16,2,16,128]{3,2,1,0:T(8,128)(2,1)S(1)} %bitcast.62, bf16[16,2,16,128]{3,2,1,0:T(8,128)(2,1)S(1)} %collective-permute-done.7.other), custom_call_target="tpu_custom_call" | custom-call | flops 1000000000 | bytes 262144 | tf_op jit(solution)/shard_map/pallas_call | solution.py:22
  98.9 0.7 fusion.4
  (25 shorter events, 0.5 us)
Async XLA Ops:
  1.6 7.3 %collective-permute-start = (bf16[2,1,8,16,128]{4,3,2,1,0:T(8,128)(2,1)S(1)}, bf16[2,1,8,16,128]{4,3,2,1,0:T(8,128)(2,1)S(1)}, u32[]{:S(2)}, u32[]{:S(2)}) collective-permute-start(bf16[2,1,8,16,128]{4,3,2,1,0:T(8,128)(2,1)S(1)} %fusion.7), channel_id=1, source_target_pairs={{16,32},{48,64},{80,96},{112,128},{144,160},{176,192},{208,224},{2... | collective-permute-start | bytes 196616 | tf_op jit(solution)/shard_map/ppermute | solution.py:287
  10.0 7.0 %copy-start = (bf16[16,3,3,3,256]{4,0,3,2,1:T(8,128)(2,1)S(1)}, bf16[16,3,3,3,256]{4,0,3,2,1:T(8,128)(2,1)}, u32[]{:S(2)}) copy-start(bf16[16,3,3,3,256]{4,0,3,2,1:T(8,128)(2,1)} %param.4) | copy-start | bytes 663556
  10.0 27.7 %all-to-all-start = ((bf16[8,3,8,16,128]{4,3,2,1,0:T(8,128)(2,1)}), bf16[8,3,8,16,128]{4,3,2,1,0:T(8,128)(2,1)S(1)}, u32[]{:S(2)}, u32[]{:S(2)}) async-start(bf16[8,3,8,16,128]{4,3,2,1,0:T(8,128)(2,1)} %broadcast_in_dim.30), calls=%async_computation | async-start | bytes 1572864 | tf_op jit(solution)/shard_map/all_to_all | solution.py:308
  17.9 13.0 %collective-permute-start.1 = (bf16[816,128]{1,0:T(8,128)(2,1)S(1)}, bf16[816,128]{1,0:T(8,128)(2,1)S(1)}, u32[]{:S(2)}, u32[]{:S(2)}) collective-permute-start(bf16[816,128]{1,0:T(8,128)(2,1)S(1)} %pad_maximum_fusion), channel_id=1, source_target_pairs={{0,1},{1,0},{2,3},{3,2},{4,5},{5,4},{6,7},{7,6},{8,9},{9,8},{10,11... | collective-permute-start | bytes 626696 | tf_op jit(solution)/shard_map/ppermute | solution.py:301
  30.9 3.2 %collective-permute-start.2 = (bf16[2,2,8,16,128]{4,3,2,1,0:T(8,128)(2,1)S(1)}, bf16[2,2,8,16,128]{4,3,2,1,0:T(8,128)(2,1)S(1)}, u32[]{:S(2)}, u32[]{:S(2)}) collective-permute-start(bf16[2,2,8,16,128]{4,3,2,1,0:T(8,128)(2,1)S(1)} %fusion.2), channel_id=1, source_target_pairs={{0,16},{16,0},{1,17},{17,1},{2,18},{18,2},{3,19},{19,3},{4,20},{20... | collective-permute-start | bytes 393224 | tf_op jit(solution)/shard_map/ppermute | solution.py:307
  37.8 4.2 %collective-permute-start.3 = (bf16[8,3,8,16,128]{4,3,2,1,0:T(8,128)(2,1)S(1)}, bf16[8,3,8,16,128]{4,3,2,1,0:T(8,128)(2,1)S(1)}, u32[]{:S(2)}, u32[]{:S(2)}) collective-permute-start(bf16[8,3,8,16,128]{4,3,2,1,0:T(8,128)(2,1)S(1)} %all-to-all-done.vown), channel_id=1, source_target_pairs={{0,16},{16,0},{1,17},{17,1},{2,18},{18,2},{3,19},{19,3},{4,20},{20... | collective-permute-start | bytes 2359304 | tf_op jit(solution)/shard_map/ppermute | solution.py:310
  45.8 22.9 %all-to-all-start.1 = ((f32[16,32,128]{2,1,0:T(8,128)}), f32[16,32,128]{2,1,0:T(8,128)S(1)}, u32[]{:S(2)}, u32[]{:S(2)}) async-start(f32[16,32,128]{2,1,0:T(8,128)} %bitcast.16), calls=%async_computation.1 | async-start | bytes 524288 | tf_op jit(solution)/shard_map/all_to_all | solution.py:332
  58.7 10.0 %collective-permute-start.4 = (f16[1040,128]{1,0:T(8,128)(2,1)S(1)}, f16[1040,128]{1,0:T(8,128)(2,1)S(1)}, u32[]{:S(2)}, u32[]{:S(2)}) collective-permute-start(f16[1040,128]{1,0:T(8,128)(2,1)S(1)} %convert_element_type.46), channel_id=1, source_target_pairs={{0,2},{2,0},{4,6},{6,4},{8,10},{10,8},{12,14},{14,12},{1,3},{3,1},... | collective-permute-start | bytes 798728 | tf_op jit(solution)/shard_map/ppermute | solution.py:319
  60.8 24.9 %collective-permute-start.5 = (f16[272,128]{1,0:T(8,128)(2,1)S(1)}, f16[272,128]{1,0:T(8,128)(2,1)S(1)}, u32[]{:S(2)}, u32[]{:S(2)}) collective-permute-start(f16[272,128]{1,0:T(8,128)(2,1)S(1)} %convert_element_type.47), channel_id=1, source_target_pairs={{0,1},{1,0},{2,3},{3,2},{4,5},{5,4},{6,7},{7,6},{8,9},{9,8},{10,11... | collective-permute-start | bytes 208904 | tf_op jit(solution)/shard_map/ppermute | solution.py:333
  69.5 11.8 %collective-permute-start.6 = (f16[528,128]{1,0:T(8,128)(2,1)S(1)}, f16[528,128]{1,0:T(8,128)(2,1)S(1)}, u32[]{:S(2)}, u32[]{:S(2)}) collective-permute-start(f16[528,128]{1,0:T(8,128)(2,1)S(1)} %pad_maximum_fusion.2), channel_id=1, source_target_pairs={{0,4},{2,6},{4,0},{6,2},{8,12},{10,14},{12,8},{14,10},{1,5},{3,7},... | collective-permute-start | bytes 405512 | tf_op jit(solution)/shard_map/ppermute | solution.py:264
  72.8 17.8 %all-to-all-start.2 = ((bf16[32,16,128]{2,1,0:T(8,128)(2,1)}), bf16[32,16,128]{2,1,0:T(8,128)(2,1)S(1)}, u32[]{:S(2)}, u32[]{:S(2)}) async-start(bf16[32,16,128]{2,1,0:T(8,128)(2,1)} %bitcast.18), calls=%async_computation.2 | async-start | bytes 262144 | tf_op jit(solution)/shard_map/all_to_all | solution.py:349
  81.4 15.5 %collective-permute-start.8 = (f16[272,128]{1,0:T(8,128)(2,1)S(1)}, f16[272,128]{1,0:T(8,128)(2,1)S(1)}, u32[]{:S(2)}, u32[]{:S(2)}) collective-permute-start(f16[272,128]{1,0:T(8,128)(2,1)S(1)} %pad_maximum_fusion.4), channel_id=1, source_target_pairs={{0,8},{2,10},{4,12},{6,14},{8,0},{10,2},{12,4},{14,6},{1,9},{3,11}... | collective-permute-start | bytes 208904 | tf_op jit(solution)/shard_map/ppermute | solution.py:344
  90.6 6.6 %collective-permute-start.7 = (bf16[16,2,16,128]{3,2,1,0:T(8,128)(2,1)S(1)}, bf16[16,2,16,128]{3,2,1,0:T(8,128)(2,1)S(1)}, u32[]{:S(2)}, u32[]{:S(2)}) collective-permute-start(bf16[16,2,16,128]{3,2,1,0:T(8,128)(2,1)S(1)} %bitcast.61), channel_id=1, source_target_pairs={{0,16},{16,0},{1,17},{17,1},{2,18},{18,2},{3,19},{19,3},{4,20},{20... | collective-permute-start | bytes 393224 | tf_op jit(solution)/shard_map/ppermute | solution.py:352
